TPU v7x, 32 devices: a whole 2x2x4 slice. The times are simulated.
32 devices in a mesh: grp: 2 (over y), row: 16 (over z, x, core).
Axes of the slice: x: 2, y: 2, z: 4, core: 2. Of those that a mesh axis runs over, the one named last changes fastest.
Arguments:
- points: bfloat16 [65536, 128], P(('grp', 'row')), as said below
- centers: bfloat16 [8192, 128], replicated, as said below
- inner_factor: bfloat16 [8192, 8192], P('row'), as said below
- outer_factor: bfloat16 [8192, 8192], P('row'), as said below
- iterate: float32 [64, 8192], P(None, 'row'), may hold values from -6 to 6
- residual: float32 [64, 8192], P(None, 'row'), as said below
- direction: float32 [64, 8192], P(None, 'row'), as said below
Outputs:
- next_iterate: float32 [64, 8192], P(None, 'row')
- next_residual: float32 [64, 8192], P(None, 'row')
- next_direction: float32 [64, 8192], P(None, 'row')
Inputs may be any that keep to these rules, and one draw needn't show every extreme that they name: `inner_factor`: upper triangular: zero below the diagonal, positive on it. `outer_factor`: upper triangular: zero below the diagonal, positive on it. `residual`: finite real values. `direction`: finite real values. `points`: finite real values. `centers`: finite real values.
All inputs are finite; a program needn't handle non-finite values.
Results may differ from a plain program's by a relative error of at most 0.0056.
Values may be sent and summed in bfloat16 or wider, within the bound.
A program may use at most 64 MiB of HBM per device.

v0:
```python
import jax
import jax.numpy as jnp
from jax import lax
from jax.sharding import PartitionSpec as P

ridge_weight = 0.5


def kernel_rows(block_points, centers, center_norms):
    point_wide = block_points.astype(jnp.float32)
    point_norms = jnp.sum(point_wide * point_wide, axis=1)
    cross_term = lax.dot_general(
        block_points, centers, (((1,), (1,)), ((), ())), preferred_element_type=jnp.float32
    )
    distance = point_norms[:, None] + center_norms[None, :] - 2.0 * cross_term
    return jnp.exp(distance * (-4.0 / block_points.shape[1])).astype(jnp.bfloat16)


def local(points, centers, inner_factor, outer_factor, iterate, residual, direction):
    contract_last = (((1,), (1,)), ((), ()))
    own_rows = inner_factor.shape[0]
    targets = direction.shape[0]
    direction_half = direction.astype(jnp.bfloat16)
    columns = inner_factor
    inner_term = lax.dot_general(
        lax.all_gather(direction_half, "row", axis=1, tiled=True),
        columns,
        contract_last,
        preferred_element_type=jnp.float32,
    )
    inner_half = inner_term.astype(jnp.bfloat16)
    columns = outer_factor
    outer_rows = lax.dot_general(
        lax.all_gather(inner_half, "row", axis=1, tiled=True),
        columns,
        contract_last,
        preferred_element_type=jnp.float32,
    )
    outer_half = lax.all_gather(outer_rows.astype(jnp.bfloat16), "row", axis=1, tiled=True)
    center_wide = centers.astype(jnp.float32)
    center_norms = jnp.sum(center_wide * center_wide, axis=1)
    local_points = points.shape[0]
    block_rows = min(512, local_points)
    point_blocks = points.reshape(local_points // block_rows, block_rows, points.shape[1])

    def one_block(carried, block_points):
        kernel_block = kernel_rows(block_points, centers, center_norms)
        fitted = lax.dot_general(
            outer_half, kernel_block, contract_last, preferred_element_type=jnp.float32
        ).astype(jnp.bfloat16)
        return (carried + jnp.dot(fitted, kernel_block, preferred_element_type=jnp.float32), None)

    partial_sums, _ = lax.scan(
        one_block, jnp.zeros((targets, centers.shape[0]), jnp.float32), point_blocks
    )
    summed_all = lax.psum(partial_sums, ("grp", "row"))
    own_normal = lax.dynamic_slice_in_dim(summed_all, lax.axis_index("row") * own_rows, own_rows, 1)
    normal_half = own_normal.astype(jnp.bfloat16)
    point_count = local_points * lax.axis_size("grp") * lax.axis_size("row")
    outer_terms = jnp.dot(normal_half, outer_factor, preferred_element_type=jnp.float32)
    shaped = (
        lax.psum_scatter(outer_terms, "row", scatter_dimension=1, tiled=True) / point_count
        + ridge_weight * inner_term
    )
    shaped_half = shaped.astype(jnp.bfloat16)
    inner_terms = jnp.dot(shaped_half, inner_factor, preferred_element_type=jnp.float32)
    operator_image = lax.psum_scatter(inner_terms, "row", scatter_dimension=1, tiled=True)
    old_norm, curvature, cross_sum, image_norm = lax.psum(
        (
            jnp.sum(residual * residual, axis=1),
            jnp.sum(direction * operator_image, axis=1),
            jnp.sum(residual * operator_image, axis=1),
            jnp.sum(operator_image * operator_image, axis=1),
        ),
        "row",
    )
    step_size = old_norm / curvature
    next_residual = residual - step_size[:, None] * operator_image
    new_norm = old_norm - 2.0 * step_size * cross_sum + step_size * step_size * image_norm
    next_iterate = iterate + step_size[:, None] * direction
    next_direction = next_residual + (new_norm / old_norm)[:, None] * direction
    return (next_iterate, next_residual, next_direction)


def solution(mesh):
    placed = (
        P(("grp", "row"), None),
        P(),
        P("row", None),
        P("row", None),
        P(None, "row"),
        P(None, "row"),
        P(None, "row"),
    )
    return jax.shard_map(
        local,
        mesh=mesh,
        in_specs=placed,
        out_specs=(P(None, "row"), P(None, "row"), P(None, "row")),
        check_vma=False,
    )
```

profile of v0, /device:TPU:0, one launch (start us, length us, event | category | flops | bytes accessed | tf_op | source)
XLA Modules:
  0.0 460.8 jit_solution(5525864594269279531)
XLA Ops:
  7.2 1.5 convert_element_type.29
  8.8 0.0 all-gather.6.cloned.1.call-start
  8.8 41.4 %all-gather.4.cloned.1.call-done = bf16[64,8192]{1,0:T(8,128)(2,1)} async-done(((bf16[64,512]{1,0:T(8,128)(2,1)}), bf16[64,8192]{1,0:T(8,128)(2,1)}) %all-gather.4.cloned.1.call-update) | async-done | bytes 1048592 | tf_op jit(solution)/shard_map/all_gather | solution.py:26
  50.3 7.0 %fusion.10 = (bf16[64,512]{1,0:T(8,128)(2,1)}, f32[64,512]{1,0:T(8,128)S(1)}) fusion(bf16[64,8192]{1,0:T(8,128)(2,1)} %all-gather.4.cloned.1.call-done, bf16[512,8192]{1,0:T(8,128)(2,1)} %param.11), kind=kOutput, calls=%fused_computation.26 | convolution fusion | flops 536903680 | bytes 9633792 | tf_op jit(solution)/shard_map/dot_general | solution.py:25
  57.3 0.0 all-gather.8.cloned.1.call-start
  57.4 36.4 %all-gather.6.cloned.1.call-done = bf16[64,8192]{1,0:T(8,128)(2,1)} async-done(((bf16[64,512]{1,0:T(8,128)(2,1)}), bf16[64,8192]{1,0:T(8,128)(2,1)}) %all-gather.6.cloned.1.call-update) | async-done | bytes 1048592 | tf_op jit(solution)/shard_map/all_gather | solution.py:34
  93.8 7.0 %convolution_convert_fusion.1 = bf16[64,512]{1,0:T(8,128)(2,1)} fusion(bf16[64,8192]{1,0:T(8,128)(2,1)} %all-gather.6.cloned.1.call-done, bf16[512,8192]{1,0:T(8,128)(2,1)} %param.12), kind=kOutput, calls=%fused_computation.8 | convolution fusion | flops 536903680 | bytes 9502720 | tf_op jit(solution)/shard_map/dot_general | solution.py:33
  100.8 0.2 reduce-scatter.3.cloned.1.call-start
  101.0 2.7 multiply_reduce_fusion.1
  103.8 33.5 %all-gather.8.cloned.1.call-done = bf16[64,8192]{1,0:T(8,128)(2,1)} async-done(((bf16[64,512]{1,0:T(8,128)(2,1)}), bf16[64,8192]{1,0:T(8,128)(2,1)}) %all-gather.8.cloned.1.call-update) | async-done | bytes 1048592 | tf_op jit(solution)/shard_map/all_gather | solution.py:39
  137.3 87.9 %while.11 = (s32[]{:T(128)}, f32[64,8192]{1,0:T(8,128)S(1)}, bf16[4,512,128]{2,1,0:T(8,128)(2,1)}, f32[8192]{0:T(1024)S(1)}, bf16[8192,128]{1,0:T(8,128)(2,1)}, ...) while((s32[]{:T(128)}, f32[64,8192]{1,0:T(8,128)S(1)}, bf16[4,512,128]{2,1,0:T(8,128)(2,1)}, ...), condition=%wide.region_5.6_spmd.clone, body=%wide.region_3.0_spmd.clone.sunk | while | flops 2169732608 | bytes 28610700 | solution.py:53
  137.3 1.0 multiply_reduce_fusion.7
  138.3 9.1 %exponential_convert_fusion.2 = bf16[512,8192]{1,0:T(8,128)(2,1)} fusion(bf16[8192,128]{1,0:T(8,128)(2,1)} %get-tuple-element.141, f32[8192]{0:T(1024)S(1)} %get-tuple-element.140, f32[512]{0:T(512)S(1)} %multiply_reduce_fusion.7, bf16[4,512,128]{2,1,0:T(8,128)(2,1)} %get-tuple-element.139, s32[]{:T(128)S(6)} %copy.12), kind=kOutput, calls=%fused_computation.clone.1 | convolution fusion | flops 1094713344 | bytes 10651652 | tf_op jit(solution)/shard_map/while/body/eval_jaxpr/dot_general | solution.py:12
  147.4 11.9 %convolution_add_fusion.2 = f32[64,8192]{1,0:T(8,128)S(1)} fusion(bf16[512,8192]{1,0:T(8,128)(2,1)} %exponential_convert_fusion.2, f32[64,8192]{1,0:T(8,128)S(1)} %get-tuple-element.130, pred[]{:T(512)S(6)} %compare.3, bf16[64,8192]{1,0:T(8,128)(2,1)S(1)} %copy-done), kind=kOutput, calls=%fused_computation.1.clone.1 | convolution fusion | flops 1074823168 | bytes 13631489 | tf_op jit(solution)/shard_map/while/body/eval_jaxpr/dot_general | solution.py:51
  159.2 1.1 multiply_reduce_fusion.7
  160.3 9.0 %exponential_convert_fusion.2 = bf16[512,8192]{1,0:T(8,128)(2,1)} fusion(bf16[8192,128]{1,0:T(8,128)(2,1)} %get-tuple-element.141, f32[8192]{0:T(1024)S(1)} %get-tuple-element.140, f32[512]{0:T(512)S(1)} %multiply_reduce_fusion.7, bf16[4,512,128]{2,1,0:T(8,128)(2,1)} %get-tuple-element.139, s32[]{:T(128)S(6)} %copy.12), kind=kOutput, calls=%fused_computation.clone.1 | convolution fusion | flops 1094713344 | bytes 10651652 | tf_op jit(solution)/shard_map/while/body/eval_jaxpr/dot_general | solution.py:12
  169.4 11.9 %convolution_add_fusion.2 = f32[64,8192]{1,0:T(8,128)S(1)} fusion(bf16[512,8192]{1,0:T(8,128)(2,1)} %exponential_convert_fusion.2, f32[64,8192]{1,0:T(8,128)S(1)} %get-tuple-element.130, pred[]{:T(512)S(6)} %compare.3, bf16[64,8192]{1,0:T(8,128)(2,1)S(1)} %copy-done), kind=kOutput, calls=%fused_computation.1.clone.1 | convolution fusion | flops 1074823168 | bytes 13631489 | tf_op jit(solution)/shard_map/while/body/eval_jaxpr/dot_general | solution.py:51
  181.2 1.1 multiply_reduce_fusion.7
  182.3 9.0 %exponential_convert_fusion.2 = bf16[512,8192]{1,0:T(8,128)(2,1)} fusion(bf16[8192,128]{1,0:T(8,128)(2,1)} %get-tuple-element.141, f32[8192]{0:T(1024)S(1)} %get-tuple-element.140, f32[512]{0:T(512)S(1)} %multiply_reduce_fusion.7, bf16[4,512,128]{2,1,0:T(8,128)(2,1)} %get-tuple-element.139, s32[]{:T(128)S(6)} %copy.12), kind=kOutput, calls=%fused_computation.clone.1 | convolution fusion | flops 1094713344 | bytes 10651652 | tf_op jit(solution)/shard_map/while/body/eval_jaxpr/dot_general | solution.py:12
  191.3 11.9 %convolution_add_fusion.2 = f32[64,8192]{1,0:T(8,128)S(1)} fusion(bf16[512,8192]{1,0:T(8,128)(2,1)} %exponential_convert_fusion.2, f32[64,8192]{1,0:T(8,128)S(1)} %get-tuple-element.130, pred[]{:T(512)S(6)} %compare.3, bf16[64,8192]{1,0:T(8,128)(2,1)S(1)} %copy-done), kind=kOutput, calls=%fused_computation.1.clone.1 | convolution fusion | flops 1074823168 | bytes 13631489 | tf_op jit(solution)/shard_map/while/body/eval_jaxpr/dot_general | solution.py:51
  203.2 1.1 multiply_reduce_fusion.7
  204.3 9.0 %exponential_convert_fusion.2 = bf16[512,8192]{1,0:T(8,128)(2,1)} fusion(bf16[8192,128]{1,0:T(8,128)(2,1)} %get-tuple-element.141, f32[8192]{0:T(1024)S(1)} %get-tuple-element.140, f32[512]{0:T(512)S(1)} %multiply_reduce_fusion.7, bf16[4,512,128]{2,1,0:T(8,128)(2,1)} %get-tuple-element.139, s32[]{:T(128)S(6)} %copy.12), kind=kOutput, calls=%fused_computation.clone.1 | convolution fusion | flops 1094713344 | bytes 10651652 | tf_op jit(solution)/shard_map/while/body/eval_jaxpr/dot_general | solution.py:12
  213.3 11.9 %convolution_add_fusion.2 = f32[64,8192]{1,0:T(8,128)S(1)} fusion(bf16[512,8192]{1,0:T(8,128)(2,1)} %exponential_convert_fusion.2, f32[64,8192]{1,0:T(8,128)S(1)} %get-tuple-element.130, pred[]{:T(512)S(6)} %compare.3, bf16[64,8192]{1,0:T(8,128)(2,1)S(1)} %copy-done), kind=kOutput, calls=%fused_computation.1.clone.1 | convolution fusion | flops 1074823168 | bytes 13631489 | tf_op jit(solution)/shard_map/while/body/eval_jaxpr/dot_general | solution.py:51
  225.2 62.9 %all-reduce.2 = bf16[64,8192]{1,0:T(8,128)(2,1)S(1)} all-reduce(f32[64,8192]{1,0:T(8,128)S(1)} %get-tuple-element.35), channel_id=1, replica_groups=mesh['grp'=2,'row'=16] {'grp','row'}, use_global_device_ids=true, to_apply=%region_6.7 | all-reduce | flops 524288 | bytes 3145728 | tf_op jit(solution)/shard_map/psum | solution.py:56
  288.1 6.3 %fusion.3 = f32[64,8192]{1,0:T(8,128)} fusion(bf16[512,8192]{1,0:T(8,128)(2,1)} %param.12, bf16[64,8192]{1,0:T(8,128)(2,1)S(1)} %all-reduce.2, s32[]{:T(128)S(6)} %select_n.3), kind=kOutput, calls=%fused_computation.18 | convolution fusion | flops 536870912 | bytes 10551300 | tf_op jit(solution)/shard_map/dot_general | solution.py:60
  294.4 0.0 reduce-scatter.5.cloned.1.call-start
  294.5 60.4 %reduce-scatter.3.cloned.1.call-done = f32[64,512]{1,0:T(8,128)} async-done(((f32[64,8192]{1,0:T(8,128)}), f32[64,512]{1,0:T(8,128)}) %reduce-scatter.3.cloned.1.call-update) | async-done | bytes 131088 | tf_op jit(solution)/shard_map/reduce_scatter | solution.py:62
  354.8 6.4 %fusion.4 = f32[64,8192]{1,0:T(8,128)} fusion(bf16[512,8192]{1,0:T(8,128)(2,1)} %param.11, f32[64,512]{1,0:T(8,128)S(1)} %get-tuple-element.83, f32[64,512]{1,0:T(8,128)} %reduce-scatter.3.cloned.1.call-done), kind=kOutput, calls=%fused_computation.19 | convolution fusion | flops 537001984 | bytes 10747904 | tf_op jit(solution)/shard_map/dot_general | solution.py:66
  361.3 60.7 %reduce-scatter.5.cloned.1.call-done = f32[64,512]{1,0:T(8,128)} async-done(((f32[64,8192]{1,0:T(8,128)}), f32[64,512]{1,0:T(8,128)}) %reduce-scatter.5.cloned.1.call-update) | async-done | bytes 131088 | tf_op jit(solution)/shard_map/reduce_scatter | solution.py:67
  421.9 1.1 multiply_reduce_fusion.3
  423.0 29.5 %all-reduce = (f32[64]{0:T(128)S(1)}, f32[64]{0:T(128)S(1)}, f32[64]{0:T(128)S(1)}, f32[64]{0:T(128)S(1)}) all-reduce(f32[64]{0:T(128)S(1)} %get-tuple-element.60, f32[64]{0:T(128)S(1)} %get-tuple-element.59, f32[64]{0:T(128)S(1)} %get-tuple-element.58, f32[64]{0:T(128)S(1)} %get-tuple-element.57), channel_id=1, replica_groups=mesh['grp'=2,'row'=16] {'row'}, use_global_device_ids=true, to_apply=%region_1.2 | all-reduce | flops 256 | bytes 2048 | tf_op jit(solution)/shard_map/psum | solution.py:68
  452.5 1.7 multiply_add_fusion
  (22 shorter events, 0.2 us)
Async XLA Ops:
  7.2 43.1 %all-gather.4.cloned.1.call-start = ((), (), s32[]{:S(2)}) async-start(), calls=%async_computation.2 | async-start | bytes 1114112 | tf_op jit(solution)/shard_map/all_gather | solution.py:26
  8.8 85.0 %all-gather.6.cloned.1.call-start = ((), (), s32[]{:S(2)}) async-start(), calls=%async_computation.3 | async-start | bytes 1114112 | tf_op jit(solution)/shard_map/all_gather | solution.py:34
  57.3 80.0 %all-gather.8.cloned.1.call-start = ((), (), s32[]{:S(2)}) async-start(), calls=%async_computation.4 | async-start | bytes 1114112 | tf_op jit(solution)/shard_map/all_gather | solution.py:39
  100.8 254.0 %reduce-scatter.3.cloned.1.call-start = ((), (), s32[]{:S(2)}) async-start(), calls=%async_computation.5 | async-start | bytes 2228224 | tf_op jit(solution)/shard_map/reduce_scatter | solution.py:62
  138.3 9.1 %copy-start = (bf16[64,8192]{1,0:T(8,128)(2,1)S(1)}, bf16[64,8192]{1,0:T(8,128)(2,1)}, u32[]{:S(2)}) copy-start(bf16[64,8192]{1,0:T(8,128)(2,1)} %get-tuple-element.142) | copy-start | bytes 3145732 | tf_op jit(solution)/shard_map/while
  160.3 9.1 %copy-start = (bf16[64,8192]{1,0:T(8,128)(2,1)S(1)}, bf16[64,8192]{1,0:T(8,128)(2,1)}, u32[]{:S(2)}) copy-start(bf16[64,8192]{1,0:T(8,128)(2,1)} %get-tuple-element.142) | copy-start | bytes 3145732 | tf_op jit(solution)/shard_map/while
  182.3 9.1 %copy-start = (bf16[64,8192]{1,0:T(8,128)(2,1)S(1)}, bf16[64,8192]{1,0:T(8,128)(2,1)}, u32[]{:S(2)}) copy-start(bf16[64,8192]{1,0:T(8,128)(2,1)} %get-tuple-element.142) | copy-start | bytes 3145732 | tf_op jit(solution)/shard_map/while
  204.3 9.1 %copy-start = (bf16[64,8192]{1,0:T(8,128)(2,1)S(1)}, bf16[64,8192]{1,0:T(8,128)(2,1)}, u32[]{:S(2)}) copy-start(bf16[64,8192]{1,0:T(8,128)(2,1)} %get-tuple-element.142) | copy-start | bytes 3145732 | tf_op jit(solution)/shard_map/while
  294.4 127.5 %reduce-scatter.5.cloned.1.call-start = ((), (), s32[]{:S(2)}) async-start(), calls=%async_computation.6 | async-start | bytes 2228224 | tf_op jit(solution)/shard_map/reduce_scatter | solution.py:67
  354.8 67.1 %copy-start.1 = (f32[64,512]{1,0:T(8,128)S(1)}, f32[64,512]{1,0:T(8,128)}, u32[]{:S(2)}) copy-start(f32[64,512]{1,0:T(8,128)} %param.15) | copy-start | bytes 393220
  354.8 67.1 %copy-start.2 = (f32[64,512]{1,0:T(8,128)S(1)}, f32[64,512]{1,0:T(8,128)}, u32[]{:S(2)}) copy-start(f32[64,512]{1,0:T(8,128)} %param.14) | copy-start | bytes 393220
  354.8 97.7 %copy-start.3 = (f32[64,512]{1,0:T(8,128)S(1)}, f32[64,512]{1,0:T(8,128)}, u32[]{:S(2)}) copy-start(f32[64,512]{1,0:T(8,128)} %param.13) | copy-start | bytes 393220
Sparse Core Ops, SparseCore 0:
  10.7 39.4 all-gather.3
  57.4 36.2 all-gather.5
  100.9 36.2 all-gather.7
  294.5 60.2 reduce-scatter.2
  361.4 60.4 reduce-scatter.4
where the time goes:
time: 461 us
  waiting for transfers between devices  232 us (50%)
  matrix products  110 us (24%)
  blocking collectives  92.4 us (20%)
  between operations  13.8 us (3%)
  other arithmetic  11.3 us (2%)
    psum x1, blocking collectives, local(): summed_all = lax.psum(partial_sums, ('grp', 'row'))  62.9 us
    reduce_scatter x1, waiting for transfers between devices, local(): lax.psum_scatter(inner_terms, 'row', scatter_dimension=1, tiled=True)  60.7 us
    reduce_scatter x1, waiting for transfers between devices, local(): lax.psum_scatter(outer_terms, 'row', scatter_dimension=1, tiled=True)  60.4 us
    dot_general x4, matrix products, one_block(): jnp.dot(fitted, kernel_block, preferred_element_type=jnp.float32)  47.4 us
    all_gather x1, waiting for transfers between devices, local(): lax.all_gather(direction_half, 'row', axis=1, tiled=True)  41.4 us
    all_gather x1, waiting for transfers between devices, local(): lax.all_gather(inner_half, 'row', axis=1, tiled=True)  36.4 us
    dot_general x4, matrix products, kernel_rows(): lax.dot_general(block_points, centers, (((1,), (1,)), ((), ())), preferre...  36.2 us
    all_gather x1, waiting for transfers between devices, local(): lax.all_gather(outer_rows.astype(jnp.bfloat16), 'row', axis=1, tiled=True)  33.5 us
  transfers between devices with their start and end apart: 5, of which 5 were waited for; matrix products, arithmetic and copies ran while one was open for 1% of the time, Pallas kernels for 0%

commit v1 on v0

v1 whole, which is shorter than its diff:
```python
import functools
import math

import jax
import jax.numpy as jnp
from jax import lax
from jax.experimental import pallas as pl
from jax.experimental.pallas import tpu as pltpu
from jax.sharding import PartitionSpec as P

ridge_weight = 0.5
MESH = pl.DeviceIdType.MESH
LAST = (((1,), (1,)), ((), ()))
f32, bf16 = jnp.float32, jnp.bfloat16

A1, A1S, A2, A2S, A3, A3S, A3Y, A3O, NC, NY, NP, O_S, O_P, I_S, I_P, CHANNELS = range(16)
Y1, Y2, YN, YS, YI, SINGLES = range(6)


def nt(a, b):
    return lax.dot_general(a, b, LAST, preferred_element_type=f32)


def mm(a, b):
    return jnp.dot(a, b, preferred_element_type=f32)


def norm_columns(wide, first, other):
    scale = 4.0 / wide.shape[1]
    norms = jnp.minimum(jnp.sum(wide * wide, axis=1, keepdims=True), 3e38) * -scale
    high = norms.astype(bf16).astype(f32)
    mid = (norms - high).astype(bf16).astype(f32)
    low = norms - high - mid
    lane = lax.broadcasted_iota(jnp.int32, wide.shape, 1)
    held = jnp.where(lane == first, high, 0.0)
    held = jnp.where(lane == first + 1, mid, held)
    held = jnp.where(lane == first + 2, low, held)
    held = jnp.where((lane >= other) & (lane < other + 3), 1.0, held)
    return held.astype(bf16)


def kernel(
    groups, n, point_count,
    points_hbm, centers_hbm, inner_hbm, outer_hbm, iterate, residual, direction,
    next_iterate, next_residual, next_direction,
    gram, inner_v, outer_v, points_v, centers_v, points_aug, centers_aug,
    half1, half2, own3, oth3, fit, fit_half, acc, ytx1, yrx1, ytx2, yrx2, inner_term,
    ctx, keep, ys, tx, nc_rx, ny_rx, np_rx, os_rx, op_rx, is_rx, ip_rx,
    normal_half, shaped_half, image, pair_sums, dots,
    lsem, ssem, rsem, ssing, rsing, psend, precv, dsend, drecv,
):
    pairs = n // 2
    own = inner_hbm.shape[0]
    targets = direction.shape[0]
    dims = points_hbm.shape[1]
    g, r = lax.axis_index("grp"), lax.axis_index("row")
    q, c, p = lax.rem(g, 2), lax.rem(r, 2), r // 2
    base = g - q
    active = c == q
    idle = c != q
    sib = (g, r + 1 - 2 * c)
    across = (g + 1 - 2 * q, r)

    def peer(k):
        return (g, 2 * k + q)

    def rc(src, dst, ch, si, ri, dev):
        return pltpu.make_async_remote_copy(
            src_ref=src, dst_ref=dst, send_sem=ssem.at[ch, si], recv_sem=rsem.at[ch, ri],
            device_id=dev, device_id_type=MESH)

    def single(src, dst, ch):
        return pltpu.make_async_remote_copy(
            src_ref=src, dst_ref=dst, send_sem=ssing.at[ch], recv_sem=rsing.at[ch],
            device_id=across, device_id_type=MESH)

    def loop(lo, hi, body):
        def step(s, carry):
            body(s)
            return carry
        lax.fori_loop(lo, hi, step, 0)

    def back(s):
        return lax.rem(p - s + 2 * pairs, pairs)

    def ahead(s):
        return lax.rem(p + 1 + s, pairs)

    points_in = pltpu.make_async_copy(points_hbm, points_v, lsem.at[2, 0])
    centers_in = pltpu.make_async_copy(centers_hbm, centers_v, lsem.at[2, 1])
    points_in.start()
    centers_in.start()

    def slab(factor, held, which, k):
        columns = pl.ds(pl.multiple_of((2 * k + q) * own, own), own)
        return pltpu.make_async_copy(factor.at[:, columns], held.at[k], lsem.at[which, k])

    loop(0, pairs, lambda s: slab(inner_hbm, inner_v, 0, back(s)).start())
    loop(0, pairs, lambda s: slab(outer_hbm, outer_v, 1, back(s)).start())

    @pl.when(active)
    def _():
        half1[p] = direction[...].astype(bf16)

    barrier = pltpu.get_barrier_semaphore()

    def greet(d):
        gg, rr = base + d // n, lax.rem(d, n)

        @pl.when((gg != g) | (rr != r))
        def _():
            pl.semaphore_signal(barrier, inc=1, device_id=(gg, rr), device_id_type=MESH)

    loop(0, 2 * n, greet)
    for h in range(groups // 2 if groups > 2 else 0):
        @pl.when(2 * h + q != g)
        def _():
            pl.semaphore_signal(barrier, inc=1, device_id=(2 * h + q, r), device_id_type=MESH)
    pl.semaphore_wait(barrier, 2 * n - 1 + groups // 2 - 1)

    def spread(half, ch):
        @pl.when(active)
        def _():
            loop(1, pairs, lambda s: rc(
                half.at[p], half.at[p], ch, lax.rem(p + s, pairs), p, peer(lax.rem(p + s, pairs))).start())
            rc(half.at[p], half.at[p], ch + 1, p, p, sib).start()

    def take(half, ch, s, k):
        @pl.when(active & (s > 0))
        def _():
            rc(half.at[k], half.at[k], ch, k, k, sib).wait_recv()
            rc(half.at[k], half.at[k], ch + 1, k, k, sib).start()

        @pl.when(idle)
        def _():
            rc(half.at[k], half.at[k], ch + 1, k, k, sib).wait_recv()

    tile = min(512, points_hbm.shape[0])

    def gram_block(b):
        rows = pl.ds(pl.multiple_of(b * own, own), own)
        block = centers_v[rows, :]
        centers_aug[:, :dims] = block
        centers_aug[:, dims:] = norm_columns(block.astype(f32), 3, 0)
        for i in range(points_hbm.shape[0] // tile):
            at = slice(i * tile, (i + 1) * tile)
            power = nt(points_aug[at, :], centers_aug[...])
            gram[b, at, :] = jnp.exp2(power * math.log2(math.e)).astype(bf16)

    spread(half1, A1)
    points_in.wait()
    for i in range(points_hbm.shape[0] // tile):
        at = slice(i * tile, (i + 1) * tile)
        block = points_v[at, :]
        wide = block.astype(f32)
        points_aug[at, :dims] = (wide * (8.0 / dims)).astype(bf16)
        points_aug[at, dims:] = norm_columns(wide, 0, 3)
    centers_in.wait()

    acc[...] = jnp.zeros_like(acc)

    def inner_step(s):
        k = back(s)
        take(half1, A1, s, k)
        slab(inner_hbm, inner_v, 0, k).wait()
        acc[...] += nt(half1[k], inner_v[k])
        gram_block(s)

    loop(0, pairs, inner_step)

    @pl.when(idle)
    def _():
        ytx1[...] = acc[...]
        single(ytx1, yrx1, Y1).start()

    @pl.when(active)
    def _():
        single(ytx1, yrx1, Y1).wait_recv()
        total = acc[...] + yrx1[...]
        inner_term[...] = total
        half2[p] = total.astype(bf16)

    spread(half2, A2)
    acc[...] = jnp.zeros_like(acc)

    def outer_step(s):
        k = back(s)
        take(half2, A2, s, k)
        slab(outer_hbm, outer_v, 1, k).wait()
        acc[...] += nt(half2[k], outer_v[k])
        gram_block(pairs + s)

    loop(0, pairs, outer_step)

    @pl.when(idle)
    def _():
        ytx2[...] = acc[...]
        single(ytx2, yrx2, Y2).start()

    @pl.when(active)
    def _():
        single(ytx2, yrx2, Y2).wait_recv()
        own3[p] = (acc[...] + yrx2[...]).astype(bf16)
        rc(own3.at[p], oth3.at[p], A3Y, p, p, across).start()

    spread(own3, A3)
    fit[...] = jnp.zeros_like(fit)

    def fit_step(s):
        k, k1, k2 = back(s), back(s - 1), back(s - 2)

        @pl.when(s < pairs)
        def _():
            take(own3, A3, s, k)

            @pl.when(active & (s > 0))
            def _():
                rc(own3.at[k], oth3.at[k], A3Y, k, k, across).start()

        @pl.when(idle & (s > 0) & (s <= pairs))
        def _():
            rc(oth3.at[k1], oth3.at[k1], A3Y, k1, k1, across).wait_recv()
            rc(oth3.at[k1], oth3.at[k1], A3O, k1, k1, sib).start()

        @pl.when(s < pairs)
        def _():
            fit[...] += nt(own3[k], gram[2 * k + q])

        @pl.when(s >= 2)
        def _():
            @pl.when(active)
            def _():
                rc(oth3.at[k2], oth3.at[k2], A3O, k2, k2, sib).wait_recv()

            fit[...] += nt(oth3[k2], gram[2 * k2 + 1 - q])

    loop(0, pairs + 2, fit_step)
    fit_half[...] = fit[...].astype(bf16)

    def normal_step(s):
        k, k1, k2 = ahead(s), ahead(s - 1 + pairs), ahead(s - 2 + pairs)

        @pl.when(s < pairs)
        def _():
            ctx[k] = mm(fit_half[...], gram[2 * k + 1 - c]).astype(bf16)
            rc(ctx.at[k], nc_rx.at[k], NC, k, k, sib).start()
            keep[k] = mm(fit_half[...], gram[2 * k + c])

        @pl.when((s >= 1) & (s <= pairs))
        def _():
            rc(ctx.at[k1], nc_rx.at[k1], NC, k1, k1, sib).wait_recv()
            total = keep[k1] + nc_rx[k1].astype(f32)

            @pl.when(idle)
            def _():
                ys[k1] = total.astype(bf16)
                rc(ys.at[k1], ny_rx.at[k1], NY, k1, k1, across).start()

            @pl.when(active)
            def _():
                keep[k1] = total

        @pl.when(active & (s >= 2))
        def _():
            rc(ys.at[k2], ny_rx.at[k2], NY, k2, k2, across).wait_recv()
            deliver(keep[k2] + ny_rx[k2].astype(f32), k2, np_rx, NP)

    def deliver(total, k, rx, ch):
        @pl.when(k != p)
        def _():
            tx[k] = total.astype(bf16)
            rc(tx.at[k], rx.at[p], ch, k, p, peer(k)).start()

        @pl.when(k == p)
        def _():
            keep[k] = total

    def collect(rx, ch):
        acc[...] = keep[p]

        def one(s):
            k = back(s)
            rc(tx.at[k], rx.at[k], ch, k, k, sib).wait_recv()
            acc[...] += rx[k].astype(f32)

        loop(1, pairs, one)

    def sent(src, ch, with_own):
        def one(k):
            if with_own:
                rc(src.at[k], src.at[k], ch, k, k, sib).wait_send()
            else:
                @pl.when(k != p)
                def _():
                    rc(src.at[k], src.at[k], ch, k, k, sib).wait_send()
        loop(0, pairs, one)

    loop(0, pairs + 2, normal_step)
    sent(ctx, NC, True)

    @pl.when(active)
    def _():
        collect(np_rx, NP)
        if groups > 2:
            mine = g // 2
            pair_sums[mine] = acc[...]

            def pair_copy(h, to):
                return pltpu.make_async_remote_copy(
                    src_ref=pair_sums.at[h], dst_ref=pair_sums.at[h], send_sem=psend.at[to],
                    recv_sem=precv.at[h], device_id=(2 * to + q, r), device_id_type=MESH)

            for h in range(groups // 2):
                @pl.when(h != mine)
                def _():
                    pair_copy(mine, h).start()
            for h in range(groups // 2):
                @pl.when(h != mine)
                def _():
                    pair_copy(h, h).wait_recv()
            total = pair_sums[0]
            for h in range(1, groups // 2):
                total = total + pair_sums[h]
            acc[...] = total
            for h in range(groups // 2):
                @pl.when(h != mine)
                def _():
                    pair_copy(mine, h).wait_send()
        normal_half[...] = acc[...].astype(bf16)
        single(normal_half, normal_half, YN).start()
        sent(tx, NP, False)

    @pl.when(idle)
    def _():
        single(normal_half, normal_half, YN).wait_recv()

    def transposed(held, lhs, s_rx, p_rx, ch_s, ch_p):
        def one(s):
            k, k1 = ahead(s), ahead(s - 1 + pairs)

            @pl.when(s < pairs)
            def _():
                term = mm(lhs[...], held[k])

                @pl.when(idle)
                def _():
                    ctx[k] = term.astype(bf16)
                    rc(ctx.at[k], s_rx.at[k], ch_s, k, k, sib).start()

                @pl.when(active)
                def _():
                    keep[k] = term

            @pl.when(active & (s >= 1))
            def _():
                rc(ctx.at[k1], s_rx.at[k1], ch_s, k1, k1, sib).wait_recv()
                deliver(keep[k1] + s_rx[k1].astype(f32), k1, p_rx, ch_p)

        loop(0, pairs + 1, one)

        @pl.when(active)
        def _():
            collect(p_rx, ch_p)
            sent(tx, ch_p, False)

        @pl.when(idle)
        def _():
            sent(ctx, ch_s, True)

    transposed(outer_v, normal_half, os_rx, op_rx, O_S, O_P)

    @pl.when(active)
    def _():
        shaped = acc[...] * (1.0 / point_count) + ridge_weight * inner_term[...]
        shaped_half[...] = shaped.astype(bf16)
        single(shaped_half, shaped_half, YS).start()

    @pl.when(idle)
    def _():
        single(shaped_half, shaped_half, YS).wait_recv()

    transposed(inner_v, shaped_half, is_rx, ip_rx, I_S, I_P)

    def dot_copy(slot, d):
        return pltpu.make_async_remote_copy(
            src_ref=dots.at[slot], dst_ref=dots.at[slot], send_sem=dsend.at[d], recv_sem=drecv.at[slot],
            device_id=(base + d // n, lax.rem(d, n)), device_id_type=MESH)

    me = q * n + r
    lane = lax.broadcasted_iota(jnp.int32, (targets, 128), 1)

    @pl.when(active)
    def _():
        image[...] = acc[...]
        x, y, z = acc[...], residual[...], direction[...]
        packed = jnp.zeros((targets, 128), f32)
        for at, pair in enumerate(((y, y), (z, x), (y, x), (x, x))):
            packed = jnp.where(lane == at, jnp.sum(pair[0] * pair[1], axis=1, keepdims=True), packed)
        square = jnp.concatenate([packed, jnp.zeros((128 - targets, 128), f32)], axis=0)
        dots[r] = square.T[:8, :]

        def one(d):
            @pl.when(d != me)
            def _():
                dot_copy(r, d).start()

        loop(0, 2 * n, one)
        single(image, image, YI).start()

    def arrived(slot):
        @pl.when(idle | (slot != r))
        def _():
            dot_copy(slot, me).wait_recv()

    loop(0, n, arrived)
    totals = dots[0]
    for slot in range(1, n):
        totals = totals + dots[slot]
    square = jnp.concatenate([totals, jnp.zeros((120, 128), f32)], axis=0).T

    @pl.when(idle)
    def _():
        single(image, image, YI).wait_recv()

    old_norm, curvature = square[:targets, 0:1], square[:targets, 1:2]
    cross_sum, image_norm = square[:targets, 2:3], square[:targets, 3:4]
    step_size = old_norm / curvature
    new_norm = old_norm - 2.0 * step_size * cross_sum + step_size * step_size * image_norm
    following = residual[...] - step_size * image[...]
    next_residual[...] = following
    next_iterate[...] = iterate[...] + step_size * direction[...]
    next_direction[...] = following + (new_norm / old_norm) * direction[...]

    @pl.when(active)
    def _():
        sent(half1, A1, False)
        sent(half1, A1S, True)
        sent(half2, A2, False)
        sent(half2, A2S, True)
        sent(own3, A3, False)
        sent(own3, A3S, True)
        sent(own3, A3Y, True)
        single(normal_half, normal_half, YN).wait_send()
        single(shaped_half, shaped_half, YS).wait_send()
        single(image, image, YI).wait_send()

        def one(d):
            @pl.when(d != me)
            def _():
                dot_copy(r, d).wait_send()

        loop(0, 2 * n, one)

    @pl.when(idle)
    def _():
        single(ytx1, yrx1, Y1).wait_send()
        single(ytx2, yrx2, Y2).wait_send()
        sent(oth3, A3O, True)
        sent(ys, NY, True)


def local(groups, n, points, centers, inner_factor, outer_factor, iterate, residual, direction):
    pairs, own = n // 2, inner_factor.shape[0]
    count, dims = points.shape
    targets = direction.shape[0]
    half = pltpu.VMEM((pairs, targets, own), bf16)
    block = pltpu.VMEM((targets, own), f32)
    slabs = pltpu.VMEM((pairs, own, own), bf16)
    vmem = pl.BlockSpec(memory_space=pltpu.VMEM)
    anywhere = pl.BlockSpec(memory_space=pl.ANY)
    dma = pltpu.SemaphoreType.DMA
    return tuple(pl.pallas_call(
        functools.partial(kernel, groups, n, count * groups * n),
        out_shape=[jax.ShapeDtypeStruct((targets, own), f32)] * 3,
        in_specs=[anywhere] * 4 + [vmem] * 3,
        out_specs=[vmem] * 3,
        scratch_shapes=[
            pltpu.VMEM((n, count, own), bf16), slabs, slabs,
            pltpu.VMEM((count, dims), bf16), pltpu.VMEM(centers.shape, bf16),
            pltpu.VMEM((count, 2 * dims), bf16), pltpu.VMEM((own, 2 * dims), bf16),
            half, half, half, half,
            pltpu.VMEM((targets, count), f32), pltpu.VMEM((targets, count), bf16),
            block, block, block, block, block, block,
            half, pltpu.VMEM((pairs, targets, own), f32), half, half,
            half, half, half, half, half, half, half,
            pltpu.VMEM((targets, own), bf16), pltpu.VMEM((targets, own), bf16), block,
            pltpu.VMEM((max(groups // 2, 1), targets, own) if groups > 2 else (1, 8, 128), f32),
            pltpu.VMEM((n, 8, 128), f32),
            dma((3, max(pairs, 2))), dma((CHANNELS, pairs)), dma((CHANNELS, pairs)),
            dma((SINGLES,)), dma((SINGLES,)),
            dma((max(groups // 2, 1),)), dma((max(groups // 2, 1),)), dma((2 * n,)), dma((n,)),
        ],
        compiler_params=pltpu.CompilerParams(
            collective_id=0, has_side_effects=True, vmem_limit_bytes=60 * 1024 * 1024
        ),
        cost_estimate=pl.CostEstimate(
            flops=2 * count * centers.shape[0] * (dims + 2 * targets),
            bytes_accessed=4 * own * centers.shape[0], transcendentals=count * centers.shape[0]),
    )(points, centers, inner_factor, outer_factor, iterate, residual, direction))


def solution(mesh):
    placed = (
        P(("grp", "row"), None), P(), P("row", None), P("row", None),
        P(None, "row"), P(None, "row"), P(None, "row"),
    )
    return jax.shard_map(
        functools.partial(local, mesh.shape["grp"], mesh.shape["row"]),
        mesh=mesh,
        in_specs=placed,
        out_specs=(P(None, "row"), P(None, "row"), P(None, "row")),
        check_vma=False,
    )
```

time: 461 us -> 112 us (0.24)
  waiting for transfers between devices: 232 us -> 0 us
  matrix products: 110 us -> 0 us
  Pallas kernels: 0 us -> 106 us
  blocking collectives: 92.4 us -> 0 us
  between operations: 13.8 us -> 0.64 us
  other arithmetic: 11.3 us -> 0 us
  local copies, waits for them, and re-layouts: 0.03 us -> 4.7 us
    reduce_scatter x2 -> x0, waiting for transfers between devices: 121 us -> none  [the longest x1 60.7 us: local(): lax.psum_scatter(inner_terms, 'row', scatter_dimension=1, tiled=True)]
    all_gather x3 -> x0, waiting for transfers between devices: 111 us -> none  [the longest x1 41.4 us: local(): lax.all_gather(direction_half, 'row', axis=1, tiled=True)]
    dot_general x12 -> x0, matrix products: 110 us -> none  [the longest x4 47.4 us: one_block(): jnp.dot(fitted, kernel_block, preferred_element_type=jnp.float32)]
    pallas_call x0 -> x1, Pallas kernels: none -> 106 us  [local(): pl.pallas_call(functools.partial(kernel, groups, n, count * groups * n),...]
    psum x2 -> x0, blocking collectives: 92.4 us -> none  [the longest x1 62.9 us: local(): summed_all = lax.psum(partial_sums, ('grp', 'row'))]
    reduce_sum x6 -> x0, other arithmetic: 8.03 us -> none  [the longest x4 4.21 us: kernel_rows(): point_norms = jnp.sum(point_wide * point_wide, axis=1)]
    unnamed x6 -> x3, local copies, waits for them, and re-layouts: 0.01 us -> 4.7 us
  transfers between devices with their start and end apart: 5 -> 0, of which waited for: 5 -> 0; matrix products, arithmetic and copies ran while one was open for 1% -> 0% of each run, Pallas kernels for 0% -> 0%
where the time goes in v1:
time: 112 us
  Pallas kernels  106 us (95%)
  local copies, waits for them, and re-layouts  4.7 us (4%)
    pallas_call x1, Pallas kernels, local(): pl.pallas_call(functools.partial(kernel, groups, n, count * groups * n),...  106 us
    unnamed x3, local copies, waits for them, and re-layouts  4.7 us

profile of v1, /device:TPU:0, one launch (start us, length us, event | category | flops | bytes accessed | tf_op | source)
XLA Modules:
  0.0 111.8 jit_solution(1788118379022275046)
XLA Ops:
  0.6 106.4 %shard_map.94 = (f32[64,512]{1,0:T(8,128)}, f32[64,512]{1,0:T(8,128)}, f32[64,512]{1,0:T(8,128)}) custom-call(bf16[2048,128]{1,0:T(8,128)(2,1)} %points_hbm.1, bf16[8192,128]{1,0:T(8,128)(2,1)} %centers_hbm.1, bf16[512,8192]{1,0:T(8,128)(2,1)} %inner_hbm.1, bf16[512,8192]{1,0:T(8,128)(2,1)} %outer_hbm.1, f32[64,512]{1,0:T(8,128)} %iterate.1, ...), custom_call_target="tpu_custom_call" | custom-call | flops 8589934592 | bytes 16777216 | tf_op jit(solution)/shard_map/pallas_call | solution.py:472
  107.1 1.6 %copy.13 = f32[64,512]{1,0:T(8,128)} copy(f32[64,512]{1,0:T(8,128)} %get-tuple-element.6) | data formatting | bytes 262144
  108.6 1.6 %copy.14 = f32[64,512]{1,0:T(8,128)} copy(f32[64,512]{1,0:T(8,128)} %get-tuple-element.7) | data formatting | bytes 262144
  110.2 1.6 %copy.15 = f32[64,512]{1,0:T(8,128)} copy(f32[64,512]{1,0:T(8,128)} %get-tuple-element.8) | data formatting | bytes 262144

commit v2 on v1

--- a/solution.py
+++ b/solution.py
@@ -1,5 +1,4 @@
 import functools
-import math
 
 import jax
 import jax.numpy as jnp
@@ -36,17 +35,16 @@
     held = jnp.where(lane == first + 1, mid, held)
     held = jnp.where(lane == first + 2, low, held)
     held = jnp.where((lane >= other) & (lane < other + 3), 1.0, held)
-    return held.astype(bf16)
+    return held
 
 
 def kernel(
     groups, n, point_count,
-    points_hbm, centers_hbm, inner_hbm, outer_hbm, iterate, residual, direction,
-    next_iterate, next_residual, next_direction,
+    points_hbm, centers_hbm, inner_hbm, outer_hbm, residual, direction, image, factors,
     gram, inner_v, outer_v, points_v, centers_v, points_aug, centers_aug,
     half1, half2, own3, oth3, fit, fit_half, acc, ytx1, yrx1, ytx2, yrx2, inner_term,
     ctx, keep, ys, tx, nc_rx, ny_rx, np_rx, os_rx, op_rx, is_rx, ip_rx,
-    normal_half, shaped_half, image, pair_sums, dots,
+    normal_half, shaped_half, pair_sums, dots,
     lsem, ssem, rsem, ssing, rsing, psend, precv, dsend, drecv,
 ):
     pairs = n // 2
@@ -140,12 +138,12 @@
     def gram_block(b):
         rows = pl.ds(pl.multiple_of(b * own, own), own)
         block = centers_v[rows, :]
-        centers_aug[:, :dims] = block
-        centers_aug[:, dims:] = norm_columns(block.astype(f32), 3, 0)
+        wide = block.astype(f32)
+        centers_aug[:dims, :] = wide.T.astype(bf16)
+        centers_aug[dims:, :] = norm_columns(wide, 3, 0).T.astype(bf16)
         for i in range(points_hbm.shape[0] // tile):
             at = slice(i * tile, (i + 1) * tile)
-            power = nt(points_aug[at, :], centers_aug[...])
-            gram[b, at, :] = jnp.exp2(power * math.log2(math.e)).astype(bf16)
+            gram[b, at, :] = jnp.exp(mm(points_aug[at, :], centers_aug[...])).astype(bf16)
 
     spread(half1, A1)
     points_in.wait()
@@ -154,7 +152,7 @@
         block = points_v[at, :]
         wide = block.astype(f32)
         points_aug[at, :dims] = (wide * (8.0 / dims)).astype(bf16)
-        points_aug[at, dims:] = norm_columns(wide, 0, 3)
+        points_aug[at, dims:] = norm_columns(wide, 0, 3).astype(bf16)
     centers_in.wait()
 
     acc[...] = jnp.zeros_like(acc)
@@ -426,10 +424,7 @@
     cross_sum, image_norm = square[:targets, 2:3], square[:targets, 3:4]
     step_size = old_norm / curvature
     new_norm = old_norm - 2.0 * step_size * cross_sum + step_size * step_size * image_norm
-    following = residual[...] - step_size * image[...]
-    next_residual[...] = following
-    next_iterate[...] = iterate[...] + step_size * direction[...]
-    next_direction[...] = following + (new_norm / old_norm) * direction[...]
+    factors[...] = jnp.where(lane == 0, step_size, new_norm / old_norm)
 
     @pl.when(active)
     def _():
@@ -459,6 +454,14 @@
         sent(ys, NY, True)
 
 
+def update(image, factors, iterate, residual, direction, next_iterate, next_residual, next_direction):
+    step_size, ratio = factors[:, 0:1], factors[:, 1:2]
+    following = residual[...] - step_size * image[...]
+    next_residual[...] = following
+    next_iterate[...] = iterate[...] + step_size * direction[...]
+    next_direction[...] = following + ratio * direction[...]
+
+
 def local(groups, n, points, centers, inner_factor, outer_factor, iterate, residual, direction):
     pairs, own = n // 2, inner_factor.shape[0]
     count, dims = points.shape
@@ -469,21 +472,21 @@
     vmem = pl.BlockSpec(memory_space=pltpu.VMEM)
     anywhere = pl.BlockSpec(memory_space=pl.ANY)
     dma = pltpu.SemaphoreType.DMA
-    return tuple(pl.pallas_call(
+    image, factors = pl.pallas_call(
         functools.partial(kernel, groups, n, count * groups * n),
-        out_shape=[jax.ShapeDtypeStruct((targets, own), f32)] * 3,
-        in_specs=[anywhere] * 4 + [vmem] * 3,
-        out_specs=[vmem] * 3,
+        out_shape=[jax.ShapeDtypeStruct((targets, own), f32), jax.ShapeDtypeStruct((targets, 128), f32)],
+        in_specs=[anywhere] * 4 + [vmem] * 2,
+        out_specs=[vmem] * 2,
         scratch_shapes=[
             pltpu.VMEM((n, count, own), bf16), slabs, slabs,
             pltpu.VMEM((count, dims), bf16), pltpu.VMEM(centers.shape, bf16),
-            pltpu.VMEM((count, 2 * dims), bf16), pltpu.VMEM((own, 2 * dims), bf16),
+            pltpu.VMEM((count, 2 * dims), bf16), pltpu.VMEM((2 * dims, own), bf16),
             half, half, half, half,
             pltpu.VMEM((targets, count), f32), pltpu.VMEM((targets, count), bf16),
             block, block, block, block, block, block,
             half, pltpu.VMEM((pairs, targets, own), f32), half, half,
             half, half, half, half, half, half, half,
-            pltpu.VMEM((targets, own), bf16), pltpu.VMEM((targets, own), bf16), block,
+            pltpu.VMEM((targets, own), bf16), pltpu.VMEM((targets, own), bf16),
             pltpu.VMEM((max(groups // 2, 1), targets, own) if groups > 2 else (1, 8, 128), f32),
             pltpu.VMEM((n, 8, 128), f32),
             dma((3, max(pairs, 2))), dma((CHANNELS, pairs)), dma((CHANNELS, pairs)),
@@ -496,7 +499,13 @@
         cost_estimate=pl.CostEstimate(
             flops=2 * count * centers.shape[0] * (dims + 2 * targets),
             bytes_accessed=4 * own * centers.shape[0], transcendentals=count * centers.shape[0]),
-    )(points, centers, inner_factor, outer_factor, iterate, residual, direction))
+    )(points, centers, inner_factor, outer_factor, residual, direction)
+    return tuple(pl.pallas_call(
+        update,
+        out_shape=[jax.ShapeDtypeStruct((targets, own), f32)] * 3,
+        in_specs=[vmem] * 5,
+        out_specs=[vmem] * 3,
+    )(image, factors, iterate, residual, direction))
 
 
 def solution(mesh):

time: 112 us -> 110 us (0.982)
  local copies, waits for them, and re-layouts: 4.7 us -> 0 us
  Pallas kernels: 106 us -> 109 us
    unnamed x3 -> x0, local copies, waits for them, and re-layouts: 4.7 us -> none
    pallas_call x0 -> x1, Pallas kernels: none -> 1.94 us  [local(): pl.pallas_call(update, out_shape=[jax.ShapeDtypeStruct((targets, own), f3...]
where the time goes in v2:
time: 110 us; the launch traced here: 109 us
  Pallas kernels  109 us (99%)
    pallas_call x1, Pallas kernels, local(): pl.pallas_call(functools.partial(kernel, groups, n, count * groups * n),...  107 us

profile of v2, /device:TPU:0, one launch (start us, length us, event | category | flops | bytes accessed | tf_op | source)
XLA Modules:
  0.0 109.5 jit_solution(15036237079446752798)
XLA Ops:
  0.6 106.9 %shard_map.94 = (f32[64,512]{1,0:T(8,128)}, f32[64,128]{1,0:T(8,128)}) custom-call(bf16[2048,128]{1,0:T(8,128)(2,1)} %points_hbm.1, bf16[8192,128]{1,0:T(8,128)(2,1)} %centers_hbm.1, bf16[512,8192]{1,0:T(8,128)(2,1)} %inner_hbm.1, bf16[512,8192]{1,0:T(8,128)(2,1)} %outer_hbm.1, f32[64,512]{1,0:T(8,128)} %residual.3, f32[64,512]{1,0:T(8,128)} %direction.3), custom_call_target="tpu_custom_call" | custom-call | flops 8589934592 | bytes 16777216 | tf_op jit(solution)/shard_map/pallas_call | solution.py:475
  107.5 1.9 %shard_map.95 = (f32[64,512]{1,0:T(8,128)}, f32[64,512]{1,0:T(8,128)}, f32[64,512]{1,0:T(8,128)}) custom-call(f32[64,512]{1,0:T(8,128)} %get-tuple-element.5.image, f32[64,128]{1,0:T(8,128)} %get-tuple-element.6.factors, f32[64,512]{1,0:T(8,128)} %iterate.1, f32[64,512]{1,0:T(8,128)} %residual.3, f32[64,512]{1,0:T(8,128)} %direction.3), custom_call_target="tpu_custom_call" | custom-call | tf_op jit(solution)/shard_map/pallas_call | solution.py:503

commit v3 on v2

v3 whole, which is shorter than its diff:
```python
import functools

import jax
import jax.numpy as jnp
from jax import lax
from jax.experimental import pallas as pl
from jax.experimental.pallas import tpu as pltpu
from jax.sharding import PartitionSpec as P

ridge_weight = 0.5
MESH = pl.DeviceIdType.MESH
LAST = (((1,), (1,)), ((), ()))
f32, bf16 = jnp.float32, jnp.bfloat16

A1, A1M, A2, A2M, A3, A3M, A3S, NC, NY, NP, O_M, O_P, I_M, I_P, CHANNELS = range(15)


def nt(a, b):
    return lax.dot_general(a, b, LAST, preferred_element_type=f32)


def mm(a, b):
    return jnp.dot(a, b, preferred_element_type=f32)


def norm_columns(wide, first, other):
    scale = 4.0 / wide.shape[1]
    norms = jnp.minimum(jnp.sum(wide * wide, axis=1, keepdims=True), 3e38) * -scale
    high = norms.astype(bf16).astype(f32)
    mid = (norms - high).astype(bf16).astype(f32)
    low = norms - high - mid
    lane = lax.broadcasted_iota(jnp.int32, wide.shape, 1)
    held = jnp.where(lane == first, high, 0.0)
    held = jnp.where(lane == first + 1, mid, held)
    held = jnp.where(lane == first + 2, low, held)
    held = jnp.where((lane >= other) & (lane < other + 3), 1.0, held)
    return held


def kernel(
    groups, n, point_count,
    points_hbm, centers_hbm, inner_hbm, outer_hbm, residual, direction, image, factors,
    gram, inner_v, outer_v, points_v, centers_v, points_aug, centers_aug,
    half1, half2, half3, fit, fit_half, acc, inner_term,
    ctx, keep, tx, nc_rx, ny_rx, np_rx, om_rx, op_rx, im_rx, ip_rx,
    normal_half, shaped_half, pair_sums, dots,
    lsem, csem, ssem, rsem, isem, psend, precv, dsend, drecv,
):
    pairs = n // 2
    own = inner_hbm.shape[0]
    targets = direction.shape[0]
    dims = points_hbm.shape[1]
    g, r = lax.axis_index("grp"), lax.axis_index("row")
    q, c, p = lax.rem(g, 2), lax.rem(r, 2), r // 2
    base = g - q
    active = c == q
    idle = c != q
    sib = (g, r + 1 - 2 * c)
    across = (g + 1 - 2 * q, r)
    mate = (g + 1 - 2 * q, r + 1 - 2 * c)

    def peer(k):
        return (g, 2 * k + q)

    def rc(src, dst, ch, si, ri, dev):
        return pltpu.make_async_remote_copy(
            src_ref=src, dst_ref=dst, send_sem=ssem.at[ch, si], recv_sem=rsem.at[ch, ri],
            device_id=dev, device_id_type=MESH)

    def loop(lo, hi, body):
        def step(s, carry):
            body(s)
            return carry
        lax.fori_loop(lo, hi, step, 0)

    def back(s):
        return lax.rem(p - s + 2 * pairs, pairs)

    def ahead(s):
        return lax.rem(p + 1 + s, pairs)

    points_in = pltpu.make_async_copy(points_hbm, points_v, csem.at[2])
    points_in.start()

    def center_copy(b):
        slot = lax.rem(b, 2)
        rows = pl.ds(pl.multiple_of(b * own, own), own)
        return pltpu.make_async_copy(centers_hbm.at[rows, :], centers_v.at[slot], csem.at[slot])

    center_copy(0).start()

    def slab(factor, held, which, b):
        columns = pl.ds(pl.multiple_of(b * own, own), own)
        return pltpu.make_async_copy(factor.at[:, columns], held.at[b], lsem.at[which, b])

    @pl.when(active)
    def _():
        def load(factor, held, which):
            def one(s):
                slab(factor, held, which, 2 * back(s) + q).start()
                slab(factor, held, which, 2 * back(s) + 1 - q).start()
            loop(0, pairs, one)

        load(inner_hbm, inner_v, 0)
        load(outer_hbm, outer_v, 1)
        half1[r] = direction[...].astype(bf16)

    barrier = pltpu.get_barrier_semaphore()

    def greet(d):
        gg, rr = base + d // n, lax.rem(d, n)

        @pl.when((gg != g) | (rr != r))
        def _():
            pl.semaphore_signal(barrier, inc=1, device_id=(gg, rr), device_id_type=MESH)

    loop(0, 2 * n, greet)
    for h in range(groups // 2 if groups > 2 else 0):
        @pl.when(2 * h + q != g)
        def _():
            pl.semaphore_signal(barrier, inc=1, device_id=(2 * h + q, r), device_id_type=MESH)
    pl.semaphore_wait(barrier, 2 * n - 1 + groups // 2 - 1)

    def spread(half, ch):
        loop(1, pairs, lambda s: rc(
            half.at[r], half.at[r], ch, lax.rem(p + s, pairs), p, peer(lax.rem(p + s, pairs))).start())
        rc(half.at[r], half.at[r], ch + 1, p, p, mate).start()

    def take_own(half, ch, s):
        b = 2 * back(s) + q

        @pl.when(s > 0)
        def _():
            rc(half.at[b], half.at[b], ch, back(s), back(s), mate).wait_recv()
            rc(half.at[b], half.at[b], ch + 1, back(s), back(s), mate).start()

    def take_other(half, ch, s):
        b = 2 * back(s) + 1 - q
        rc(half.at[b], half.at[b], ch + 1, back(s), back(s), mate).wait_recv()

    tile = min(512, points_hbm.shape[0])

    def gram_block(b):
        @pl.when(b + 1 < n)
        def _():
            center_copy(b + 1).start()

        center_copy(b).wait()
        wide = centers_v[lax.rem(b, 2)].astype(f32)
        centers_aug[:dims, :] = wide.T.astype(bf16)
        centers_aug[dims:, :] = norm_columns(wide, 3, 0).T.astype(bf16)
        for i in range(points_hbm.shape[0] // tile):
            at = slice(i * tile, (i + 1) * tile)
            gram[b, at, :] = jnp.exp(mm(points_aug[at, :], centers_aug[...])).astype(bf16)

    @pl.when(active)
    def _():
        spread(half1, A1)

    points_in.wait()
    for i in range(points_hbm.shape[0] // tile):
        at = slice(i * tile, (i + 1) * tile)
        block = points_v[at, :]
        wide = block.astype(f32)
        points_aug[at, :dims] = (wide * (8.0 / dims)).astype(bf16)
        points_aug[at, dims:] = norm_columns(wide, 0, 3).astype(bf16)

    def product(half, held, which, ch, first):
        acc[...] = jnp.zeros_like(acc)

        def one(s):
            @pl.when(active & (s < pairs))
            def _():
                take_own(half, ch, s)
                b = 2 * back(s) + q
                slab(inner_hbm, held, which, b).wait()
                acc[...] += nt(half[b], held[b])

            @pl.when(active & (s >= 2))
            def _():
                take_other(half, ch, s - 2)
                b = 2 * back(s - 2) + 1 - q
                slab(inner_hbm, held, which, b).wait()
                acc[...] += nt(half[b], held[b])

            @pl.when(s < pairs)
            def _():
                gram_block(first + s)

        loop(0, pairs + 2, one)

    product(half1, inner_v, 0, A1, 0)

    @pl.when(active)
    def _():
        inner_term[...] = acc[...]
        half2[r] = acc[...].astype(bf16)
        spread(half2, A2)

    product(half2, outer_v, 1, A2, pairs)

    @pl.when(active)
    def _():
        half3[r] = acc[...].astype(bf16)
        spread(half3, A3)

    fit[...] = jnp.zeros_like(fit)

    def fit_step(s):
        def chip(b):
            copy = rc(half3.at[b], half3.at[b], A3S, b, b, sib)

            @pl.when(active)
            def _():
                copy.start()

            @pl.when(idle)
            def _():
                copy.wait_recv()

            fit[...] += nt(half3[b], gram[b])

        @pl.when(s < pairs)
        def _():
            @pl.when(active)
            def _():
                take_own(half3, A3, s)

            chip(2 * back(s) + q)

        @pl.when(s >= 2)
        def _():
            @pl.when(active)
            def _():
                take_other(half3, A3, s - 2)

            chip(2 * back(s - 2) + 1 - q)

    loop(0, pairs + 2, fit_step)
    fit_half[...] = fit[...].astype(bf16)

    def normal_step(s):
        k, k1, k2 = ahead(s), ahead(s - 1 + pairs), ahead(s - 2 + pairs)

        @pl.when(s < pairs)
        def _():
            ctx[k] = mm(fit_half[...], gram[2 * k + 1 - c]).astype(bf16)
            rc(ctx.at[k], nc_rx.at[k], NC, k, k, sib).start()
            keep[k] = mm(fit_half[...], gram[2 * k + c])

        @pl.when((s >= 1) & (s <= pairs))
        def _():
            rc(ctx.at[k1], nc_rx.at[k1], NC, k1, k1, sib).wait_recv()
            total = keep[k1] + nc_rx[k1].astype(f32)

            @pl.when(idle)
            def _():
                tx[k1] = total.astype(bf16)
                rc(tx.at[k1], ny_rx.at[k1], NY, k1, k1, across).start()

            @pl.when(active)
            def _():
                keep[k1] = total

        @pl.when(active & (s >= 2))
        def _():
            rc(tx.at[k2], ny_rx.at[k2], NY, k2, k2, across).wait_recv()
            deliver(keep[k2] + ny_rx[k2].astype(f32), k2, np_rx, NP)

    def deliver(total, k, rx, ch):
        @pl.when(k != p)
        def _():
            tx[k] = total.astype(bf16)
            rc(tx.at[k], rx.at[p], ch, k, p, peer(k)).start()

        @pl.when(k == p)
        def _():
            keep[k] = total

    def collect(rx, ch):
        acc[...] = keep[p]

        def one(s):
            k = back(s)
            rc(tx.at[k], rx.at[k], ch, k, k, sib).wait_recv()
            acc[...] += rx[k].astype(f32)

        loop(1, pairs, one)

    def sent(src, ch, with_own):
        def one(k):
            if with_own:
                rc(src.at[k], src.at[k], ch, k, k, sib).wait_send()
            else:
                @pl.when(k != p)
                def _():
                    rc(src.at[k], src.at[k], ch, k, k, sib).wait_send()
        loop(0, pairs, one)

    loop(0, pairs + 2, normal_step)
    sent(ctx, NC, True)

    @pl.when(active)
    def _():
        collect(np_rx, NP)
        if groups > 2:
            mine = g // 2
            pair_sums[mine] = acc[...]

            def pair_copy(h, to):
                return pltpu.make_async_remote_copy(
                    src_ref=pair_sums.at[h], dst_ref=pair_sums.at[h], send_sem=psend.at[to],
                    recv_sem=precv.at[h], device_id=(2 * to + q, r), device_id_type=MESH)

            for h in range(groups // 2):
                @pl.when(h != mine)
                def _():
                    pair_copy(mine, h).start()
            for h in range(groups // 2):
                @pl.when(h != mine)
                def _():
                    pair_copy(h, h).wait_recv()
            total = pair_sums[0]
            for h in range(1, groups // 2):
                total = total + pair_sums[h]
            acc[...] = total
            for h in range(groups // 2):
                @pl.when(h != mine)
                def _():
                    pair_copy(mine, h).wait_send()
        sent(tx, NP, False)
        normal_half[...] = acc[...].astype(bf16)

    def transposed(held, lhs, m_rx, p_rx, ch_m, ch_p):
        def one(s):
            k, k1 = ahead(s), ahead(s - 1 + pairs)

            @pl.when(s < pairs)
            def _():
                ctx[k] = mm(lhs[...], held[2 * k + 1 - q]).astype(bf16)
                rc(ctx.at[k], m_rx.at[k], ch_m, k, k, mate).start()
                keep[k] = mm(lhs[...], held[2 * k + q])

            @pl.when(s >= 1)
            def _():
                rc(ctx.at[k1], m_rx.at[k1], ch_m, k1, k1, mate).wait_recv()
                deliver(keep[k1] + m_rx[k1].astype(f32), k1, p_rx, ch_p)

        loop(0, pairs + 1, one)
        collect(p_rx, ch_p)
        sent(tx, ch_p, False)
        sent(ctx, ch_m, True)

    @pl.when(active)
    def _():
        transposed(outer_v, normal_half, om_rx, op_rx, O_M, O_P)
        shaped = acc[...] * (1.0 / point_count) + ridge_weight * inner_term[...]
        shaped_half[...] = shaped.astype(bf16)
        transposed(inner_v, shaped_half, im_rx, ip_rx, I_M, I_P)

    def dot_copy(slot, d):
        return pltpu.make_async_remote_copy(
            src_ref=dots.at[slot], dst_ref=dots.at[slot], send_sem=dsend.at[d], recv_sem=drecv.at[slot],
            device_id=(base + d // n, lax.rem(d, n)), device_id_type=MESH)

    image_copy = pltpu.make_async_remote_copy(
        src_ref=image, dst_ref=image, send_sem=isem.at[0], recv_sem=isem.at[1], device_id=across, device_id_type=MESH)
    me = q * n + r
    lane = lax.broadcasted_iota(jnp.int32, (targets, 128), 1)

    @pl.when(active)
    def _():
        image[...] = acc[...]
        x, y, z = acc[...], residual[...], direction[...]
        packed = jnp.zeros((targets, 128), f32)
        for at, pair in enumerate(((y, y), (z, x), (y, x), (x, x))):
            packed = jnp.where(lane == at, jnp.sum(pair[0] * pair[1], axis=1, keepdims=True), packed)
        square = jnp.concatenate([packed, jnp.zeros((128 - targets, 128), f32)], axis=0)
        dots[r] = square.T[:8, :]

        def one(d):
            @pl.when(d != me)
            def _():
                dot_copy(r, d).start()

        loop(0, 2 * n, one)
        image_copy.start()

    def arrived(slot):
        @pl.when(idle | (slot != r))
        def _():
            dot_copy(slot, me).wait_recv()

    loop(0, n, arrived)
    totals = dots[0]
    for slot in range(1, n):
        totals = totals + dots[slot]
    square = jnp.concatenate([totals, jnp.zeros((120, 128), f32)], axis=0).T

    @pl.when(idle)
    def _():
        image_copy.wait_recv()

    old_norm, curvature = square[:targets, 0:1], square[:targets, 1:2]
    cross_sum, image_norm = square[:targets, 2:3], square[:targets, 3:4]
    step_size = old_norm / curvature
    new_norm = old_norm - 2.0 * step_size * cross_sum + step_size * step_size * image_norm
    factors[...] = jnp.where(lane == 0, step_size, new_norm / old_norm)

    @pl.when(active)
    def _():
        sent(half1, A1, False)
        sent(half1, A1M, True)
        sent(half2, A2, False)
        sent(half2, A2M, True)
        sent(half3, A3, False)
        sent(half3, A3M, True)
        loop(0, n, lambda b: rc(half3.at[b], half3.at[b], A3S, b, b, sib).wait_send())
        image_copy.wait_send()

        def one(d):
            @pl.when(d != me)
            def _():
                dot_copy(r, d).wait_send()

        loop(0, 2 * n, one)

    @pl.when(idle)
    def _():
        sent(tx, NY, True)


def update(image, factors, iterate, residual, direction, next_iterate, next_residual, next_direction):
    step_size, ratio = factors[:, 0:1], factors[:, 1:2]
    following = residual[...] - step_size * image[...]
    next_residual[...] = following
    next_iterate[...] = iterate[...] + step_size * direction[...]
    next_direction[...] = following + ratio * direction[...]


def local(groups, n, points, centers, inner_factor, outer_factor, iterate, residual, direction):
    pairs, own = n // 2, inner_factor.shape[0]
    count, dims = points.shape
    targets = direction.shape[0]
    half = pltpu.VMEM((pairs, targets, own), bf16)
    block = pltpu.VMEM((targets, own), f32)
    slabs = pltpu.VMEM((n, own, own), bf16)
    whole = pltpu.VMEM((n, targets, own), bf16)
    vmem = pl.BlockSpec(memory_space=pltpu.VMEM)
    anywhere = pl.BlockSpec(memory_space=pl.ANY)
    dma = pltpu.SemaphoreType.DMA
    image, factors = pl.pallas_call(
        functools.partial(kernel, groups, n, count * groups * n),
        out_shape=[jax.ShapeDtypeStruct((targets, own), f32), jax.ShapeDtypeStruct((targets, 128), f32)],
        in_specs=[anywhere] * 4 + [vmem] * 2,
        out_specs=[vmem] * 2,
        scratch_shapes=[
            pltpu.VMEM((n, count, own), bf16), slabs, slabs,
            pltpu.VMEM((count, dims), bf16), pltpu.VMEM((2, own, dims), bf16),
            pltpu.VMEM((count, 2 * dims), bf16), pltpu.VMEM((2 * dims, own), bf16),
            whole, whole, whole,
            pltpu.VMEM((targets, count), f32), pltpu.VMEM((targets, count), bf16), block, block,
            half, pltpu.VMEM((pairs, targets, own), f32), half,
            half, half, half, half, half, half, half,
            pltpu.VMEM((targets, own), bf16), pltpu.VMEM((targets, own), bf16),
            pltpu.VMEM((groups // 2, targets, own) if groups > 2 else (1, 8, 128), f32),
            pltpu.VMEM((n, 8, 128), f32),
            dma((2, n)), dma((3,)), dma((CHANNELS, n)), dma((CHANNELS, n)), dma((2,)),
            dma((max(groups // 2, 1),)), dma((max(groups // 2, 1),)), dma((2 * n,)), dma((n,)),
        ],
        compiler_params=pltpu.CompilerParams(
            collective_id=0, has_side_effects=True, vmem_limit_bytes=63 * 1024 * 1024
        ),
        cost_estimate=pl.CostEstimate(
            flops=2 * count * centers.shape[0] * (dims + 2 * targets),
            bytes_accessed=4 * own * centers.shape[0], transcendentals=count * centers.shape[0]),
    )(points, centers, inner_factor, outer_factor, residual, direction)
    return tuple(pl.pallas_call(
        update,
        out_shape=[jax.ShapeDtypeStruct((targets, own), f32)] * 3,
        in_specs=[vmem] * 5,
        out_specs=[vmem] * 3,
    )(image, factors, iterate, residual, direction))


def solution(mesh):
    placed = (
        P(("grp", "row"), None), P(), P("row", None), P("row", None),
        P(None, "row"), P(None, "row"), P(None, "row"),
    )
    return jax.shard_map(
        functools.partial(local, mesh.shape["grp"], mesh.shape["row"]),
        mesh=mesh,
        in_specs=placed,
        out_specs=(P(None, "row"), P(None, "row"), P(None, "row")),
        check_vma=False,
    )
```

time: 110 us -> 119 us (1.082)
  Pallas kernels: 109 us -> 119 us
    pallas_call x1, Pallas kernels: 107 us -> 117 us  [local(): pl.pallas_call(functools.partial(kernel, groups, n, count * groups * n),...]
where the time goes in v3:
time: 119 us
  Pallas kernels  119 us (100%)
    pallas_call x1, Pallas kernels, local(): pl.pallas_call(functools.partial(kernel, groups, n, count * groups * n),...  117 us

profile of v3, /device:TPU:0, one launch (start us, length us, event | category | flops | bytes accessed | tf_op | source)
XLA Modules:
  0.0 119.3 jit_solution(13007479771127471627)
XLA Ops:
  0.6 116.7 %shard_map.94 = (f32[64,512]{1,0:T(8,128)}, f32[64,128]{1,0:T(8,128)}) custom-call(bf16[2048,128]{1,0:T(8,128)(2,1)} %points_hbm.1, bf16[8192,128]{1,0:T(8,128)(2,1)} %centers_hbm.1, bf16[512,8192]{1,0:T(8,128)(2,1)} %inner_hbm.1, bf16[512,8192]{1,0:T(8,128)(2,1)} %outer_hbm.1, f32[64,512]{1,0:T(8,128)} %residual.3, f32[64,512]{1,0:T(8,128)} %direction.3), custom_call_target="tpu_custom_call" | custom-call | flops 8589934592 | bytes 16777216 | tf_op jit(solution)/shard_map/pallas_call | solution.py:452
  117.3 1.9 %shard_map.95 = (f32[64,512]{1,0:T(8,128)}, f32[64,512]{1,0:T(8,128)}, f32[64,512]{1,0:T(8,128)}) custom-call(f32[64,512]{1,0:T(8,128)} %get-tuple-element.5.image, f32[64,128]{1,0:T(8,128)} %get-tuple-element.6.factors, f32[64,512]{1,0:T(8,128)} %iterate.1, f32[64,512]{1,0:T(8,128)} %residual.3, f32[64,512]{1,0:T(8,128)} %direction.3), custom_call_target="tpu_custom_call" | custom-call | tf_op jit(solution)/shard_map/pallas_call | solution.py:478

commit v4 on v2

--- a/solution.py
+++ b/solution.py
@@ -12,7 +12,10 @@
 LAST = (((1,), (1,)), ((), ()))
 f32, bf16 = jnp.float32, jnp.bfloat16
 
-A1, A1S, A2, A2S, A3, A3S, A3Y, A3O, NC, NY, NP, O_S, O_P, I_S, I_P, CHANNELS = range(16)
+(
+    A1, A1X, A1S, A2, A2X, A2S, A3, A3X, A3S, A3Y, A3O, A3OX,
+    NC, NY, NX, NP, O_S, O_X, O_P, I_S, I_X, I_P, CHANNELS,
+) = range(23)
 Y1, Y2, YN, YS, YI, SINGLES = range(6)
 
 
@@ -43,7 +46,7 @@
     points_hbm, centers_hbm, inner_hbm, outer_hbm, residual, direction, image, factors,
     gram, inner_v, outer_v, points_v, centers_v, points_aug, centers_aug,
     half1, half2, own3, oth3, fit, fit_half, acc, ytx1, yrx1, ytx2, yrx2, inner_term,
-    ctx, keep, ys, tx, nc_rx, ny_rx, np_rx, os_rx, op_rx, is_rx, ip_rx,
+    ctx, keep, ys, tx, nc_rx, ny_rx, nx_rx, np_rx, os_rx, ox_rx, op_rx, is_rx, ix_rx, ip_rx,
     normal_half, shaped_half, pair_sums, dots,
     lsem, ssem, rsem, ssing, rsing, psend, precv, dsend, drecv,
 ):
@@ -59,8 +62,17 @@
     sib = (g, r + 1 - 2 * c)
     across = (g + 1 - 2 * q, r)
 
+    rungs, z, x = pairs // 2, p // 2, lax.rem(p, 2)
+    beside = 2 * z + 1 - x
+
     def peer(k):
-        return (g, 2 * k + q)
+        return (g, 2 * k + c)
+
+    def column(j):
+        return 2 * lax.rem(z + j + 2 * rungs, rungs) + x
+
+    def next_column(j):
+        return 2 * lax.rem(z + j + 2 * rungs, rungs) + 1 - x
 
     def rc(src, dst, ch, si, ri, dev):
         return pltpu.make_async_remote_copy(
@@ -78,12 +90,6 @@
             return carry
         lax.fori_loop(lo, hi, step, 0)
 
-    def back(s):
-        return lax.rem(p - s + 2 * pairs, pairs)
-
-    def ahead(s):
-        return lax.rem(p + 1 + s, pairs)
-
     points_in = pltpu.make_async_copy(points_hbm, points_v, lsem.at[2, 0])
     centers_in = pltpu.make_async_copy(centers_hbm, centers_v, lsem.at[2, 1])
     points_in.start()
@@ -93,8 +99,12 @@
         columns = pl.ds(pl.multiple_of((2 * k + q) * own, own), own)
         return pltpu.make_async_copy(factor.at[:, columns], held.at[k], lsem.at[which, k])
 
-    loop(0, pairs, lambda s: slab(inner_hbm, inner_v, 0, back(s)).start())
-    loop(0, pairs, lambda s: slab(outer_hbm, outer_v, 1, back(s)).start())
+    def load(factor, held, which, s):
+        slab(factor, held, which, column(-s)).start()
+        slab(factor, held, which, next_column(-s)).start()
+
+    loop(0, rungs, lambda s: load(inner_hbm, inner_v, 0, s))
+    loop(0, rungs, lambda s: load(outer_hbm, outer_v, 1, s))
 
     @pl.when(active)
     def _():
@@ -119,19 +129,34 @@
     def spread(half, ch):
         @pl.when(active)
         def _():
-            loop(1, pairs, lambda s: rc(
-                half.at[p], half.at[p], ch, lax.rem(p + s, pairs), p, peer(lax.rem(p + s, pairs))).start())
-            rc(half.at[p], half.at[p], ch + 1, p, p, sib).start()
-
-    def take(half, ch, s, k):
+            rc(half.at[p], half.at[p], ch + 1, p, p, peer(beside)).start()
+            loop(1, rungs, lambda j: rc(half.at[p], half.at[p], ch, column(j), p, peer(column(j))).start())
+            rc(half.at[p], half.at[p], ch + 2, p, p, sib).start()
+
+    def take_column(half, ch, s):
+        k = column(-s)
+
         @pl.when(active & (s > 0))
         def _():
             rc(half.at[k], half.at[k], ch, k, k, sib).wait_recv()
-            rc(half.at[k], half.at[k], ch + 1, k, k, sib).start()
+            rc(half.at[k], half.at[k], ch + 1, k, k, peer(beside)).start()
+            rc(half.at[k], half.at[k], ch + 2, k, k, sib).start()
 
         @pl.when(idle)
         def _():
+            rc(half.at[k], half.at[k], ch + 2, k, k, sib).wait_recv()
+
+    def take_next(half, ch, s):
+        k = next_column(-s)
+
+        @pl.when(active)
+        def _():
             rc(half.at[k], half.at[k], ch + 1, k, k, sib).wait_recv()
+            rc(half.at[k], half.at[k], ch + 2, k, k, sib).start()
+
+        @pl.when(idle)
+        def _():
+            rc(half.at[k], half.at[k], ch + 2, k, k, sib).wait_recv()
 
     tile = min(512, points_hbm.shape[0])
 
@@ -155,16 +180,32 @@
         points_aug[at, dims:] = norm_columns(wide, 0, 3).astype(bf16)
     centers_in.wait()
 
-    acc[...] = jnp.zeros_like(acc)
-
-    def inner_step(s):
-        k = back(s)
-        take(half1, A1, s, k)
-        slab(inner_hbm, inner_v, 0, k).wait()
-        acc[...] += nt(half1[k], inner_v[k])
-        gram_block(s)
-
-    loop(0, pairs, inner_step)
+    def product(half, factor, held, which, ch, first):
+        acc[...] = jnp.zeros_like(acc)
+
+        def add(k):
+            slab(factor, held, which, k).wait()
+            acc[...] += nt(half[k], held[k])
+
+        def one(s):
+            @pl.when(s < rungs)
+            def _():
+                take_column(half, ch, s)
+                add(column(-s))
+                gram_block(first + 2 * s)
+
+            @pl.when(s > 0)
+            def _():
+                take_next(half, ch, s - 1)
+                add(next_column(1 - s))
+
+            @pl.when(s < rungs)
+            def _():
+                gram_block(first + 2 * s + 1)
+
+        loop(0, rungs + 1, one)
+
+    product(half1, inner_hbm, inner_v, 0, A1, 0)
 
     @pl.when(idle)
     def _():
@@ -179,16 +220,7 @@
         half2[p] = total.astype(bf16)
 
     spread(half2, A2)
-    acc[...] = jnp.zeros_like(acc)
-
-    def outer_step(s):
-        k = back(s)
-        take(half2, A2, s, k)
-        slab(outer_hbm, outer_v, 1, k).wait()
-        acc[...] += nt(half2[k], outer_v[k])
-        gram_block(pairs + s)
-
-    loop(0, pairs, outer_step)
+    product(half2, outer_hbm, outer_v, 1, A2, pairs)
 
     @pl.when(idle)
     def _():
@@ -204,39 +236,71 @@
     spread(own3, A3)
     fit[...] = jnp.zeros_like(fit)
 
+    def over_x(k):
+        return (lax.rem(k, 2) != x) & (lax.rem(k // 2, 2) == 1)
+
+    def to_other(k):
+        @pl.when(active & (k != p) & jnp.logical_not(over_x(k)))
+        def _():
+            rc(own3.at[k], oth3.at[k], A3Y, k, k, across).start()
+
+    def take_other(k):
+        @pl.when(idle)
+        def _():
+            @pl.when(over_x(k))
+            def _():
+                rc(oth3.at[k], oth3.at[k], A3OX, k, k, sib).wait_recv()
+
+            @pl.when(jnp.logical_not(over_x(k)))
+            def _():
+                rc(oth3.at[k], oth3.at[k], A3Y, k, k, sib).wait_recv()
+
+            @pl.when((lax.rem(k, 2) == x) & (lax.rem(k // 2, 2) == 1))
+            def _():
+                rc(oth3.at[k], oth3.at[k], A3OX, k, k, peer(beside)).start()
+
+            rc(oth3.at[k], oth3.at[k], A3O, k, k, sib).start()
+
+        @pl.when(active)
+        def _():
+            rc(oth3.at[k], oth3.at[k], A3O, k, k, sib).wait_recv()
+
     def fit_step(s):
-        k, k1, k2 = back(s), back(s - 1), back(s - 2)
-
-        @pl.when(s < pairs)
-        def _():
-            take(own3, A3, s, k)
-
-            @pl.when(active & (s > 0))
-            def _():
-                rc(own3.at[k], oth3.at[k], A3Y, k, k, across).start()
-
-        @pl.when(idle & (s > 0) & (s <= pairs))
-        def _():
-            rc(oth3.at[k1], oth3.at[k1], A3Y, k1, k1, across).wait_recv()
-            rc(oth3.at[k1], oth3.at[k1], A3O, k1, k1, sib).start()
-
-        @pl.when(s < pairs)
-        def _():
+        @pl.when(s < rungs)
+        def _():
+            k = column(-s)
+            take_column(own3, A3, s)
+            to_other(k)
             fit[...] += nt(own3[k], gram[2 * k + q])
 
+        @pl.when((s >= 1) & (s <= rungs))
+        def _():
+            k = next_column(1 - s)
+            take_next(own3, A3, s - 1)
+            to_other(k)
+            fit[...] += nt(own3[k], gram[2 * k + q])
+
+        def other(k):
+            take_other(k)
+            fit[...] += nt(oth3[k], gram[2 * k + 1 - q])
+
+        @pl.when((s >= 1) & (s <= rungs))
+        def _():
+            other(column(1 - s))
+
         @pl.when(s >= 2)
         def _():
-            @pl.when(active)
-            def _():
-                rc(oth3.at[k2], oth3.at[k2], A3O, k2, k2, sib).wait_recv()
-
-            fit[...] += nt(oth3[k2], gram[2 * k2 + 1 - q])
-
-    loop(0, pairs + 2, fit_step)
+            other(next_column(2 - s))
+
+    loop(0, rungs + 2, fit_step)
     fit_half[...] = fit[...].astype(bf16)
 
+    def turn(s):
+        j = lax.rem(z + 1 + lax.rem(s, rungs), rungs)
+        return 2 * j + jnp.where(s < rungs, 1 - x, x)
+
     def normal_step(s):
-        k, k1, k2 = ahead(s), ahead(s - 1 + pairs), ahead(s - 2 + pairs)
+        k, k1, k2 = turn(s), turn(jnp.maximum(s - 1, 0)), turn(jnp.maximum(s - 2, 0))
 
         @pl.when(s < pairs)
         def _():
@@ -261,44 +325,53 @@
         @pl.when(active & (s >= 2))
         def _():
             rc(ys.at[k2], ny_rx.at[k2], NY, k2, k2, across).wait_recv()
-            deliver(keep[k2] + ny_rx[k2].astype(f32), k2, np_rx, NP)
-
-    def deliver(total, k, rx, ch):
-        @pl.when(k != p)
+            deliver(keep[k2] + ny_rx[k2].astype(f32), k2, nx_rx, np_rx, NX)
+
+    def deliver(total, k, x_rx, rx, ch):
+        @pl.when(lax.rem(k, 2) != x)
         def _():
             tx[k] = total.astype(bf16)
-            rc(tx.at[k], rx.at[p], ch, k, p, peer(k)).start()
-
-        @pl.when(k == p)
-        def _():
-            keep[k] = total
+            rc(tx.at[k], x_rx.at[k], ch, k, k, peer(beside)).start()
+
+        @pl.when(lax.rem(k, 2) == x)
+        def _():
+            rc(tx.at[k], x_rx.at[k], ch, k, k, peer(beside)).wait_recv()
+            both = total + x_rx[k].astype(f32)
+
+            @pl.when(k != p)
+            def _():
+                tx[k] = both.astype(bf16)
+                rc(tx.at[k], rx.at[p], ch + 1, k, p, peer(k)).start()
+
+            @pl.when(k == p)
+            def _():
+                keep[k] = both
 
     def collect(rx, ch):
         acc[...] = keep[p]
 
-        def one(s):
-            k = back(s)
-            rc(tx.at[k], rx.at[k], ch, k, k, sib).wait_recv()
+        def one(j):
+            k = column(-j)
+            rc(tx.at[k], rx.at[k], ch + 1, k, k, sib).wait_recv()
             acc[...] += rx[k].astype(f32)
 
-        loop(1, pairs, one)
-
-    def sent(src, ch, with_own):
-        def one(k):
-            if with_own:
-                rc(src.at[k], src.at[k], ch, k, k, sib).wait_send()
-            else:
-                @pl.when(k != p)
-                def _():
-                    rc(src.at[k], src.at[k], ch, k, k, sib).wait_send()
-        loop(0, pairs, one)
+        loop(1, rungs, one)
+
+    def delivered(ch):
+        loop(0, rungs, lambda j: rc(
+            tx.at[next_column(j)], tx.at[next_column(j)], ch, next_column(j), p, sib).wait_send())
+        loop(1, rungs, lambda j: rc(
+            tx.at[column(j)], tx.at[column(j)], ch + 1, column(j), p, sib).wait_send())
+
+    def sent(src, ch):
+        loop(0, pairs, lambda k: rc(src.at[k], src.at[k], ch, k, k, sib).wait_send())
 
     loop(0, pairs + 2, normal_step)
-    sent(ctx, NC, True)
+    sent(ctx, NC)
 
     @pl.when(active)
     def _():
-        collect(np_rx, NP)
+        collect(np_rx, NX)
         if groups > 2:
             mine = g // 2
             pair_sums[mine] = acc[...]
@@ -326,15 +399,15 @@
                     pair_copy(mine, h).wait_send()
         normal_half[...] = acc[...].astype(bf16)
         single(normal_half, normal_half, YN).start()
-        sent(tx, NP, False)
+        delivered(NX)
 
     @pl.when(idle)
     def _():
         single(normal_half, normal_half, YN).wait_recv()
 
-    def transposed(held, lhs, s_rx, p_rx, ch_s, ch_p):
+    def transposed(held, lhs, s_rx, x_rx, p_rx, ch_s):
         def one(s):
-            k, k1 = ahead(s), ahead(s - 1 + pairs)
+            k, k1 = turn(s), turn(jnp.maximum(s - 1, 0))
 
             @pl.when(s < pairs)
             def _():
@@ -352,20 +425,20 @@
             @pl.when(active & (s >= 1))
             def _():
                 rc(ctx.at[k1], s_rx.at[k1], ch_s, k1, k1, sib).wait_recv()
-                deliver(keep[k1] + s_rx[k1].astype(f32), k1, p_rx, ch_p)
+                deliver(keep[k1] + s_rx[k1].astype(f32), k1, x_rx, p_rx, ch_s + 1)
 
         loop(0, pairs + 1, one)
 
         @pl.when(active)
         def _():
-            collect(p_rx, ch_p)
-            sent(tx, ch_p, False)
+            collect(p_rx, ch_s + 1)
+            delivered(ch_s + 1)
 
         @pl.when(idle)
         def _():
-            sent(ctx, ch_s, True)
-
-    transposed(outer_v, normal_half, os_rx, op_rx, O_S, O_P)
+            sent(ctx, ch_s)
+
+    transposed(outer_v, normal_half, os_rx, ox_rx, op_rx, O_S)
 
     @pl.when(active)
     def _():
@@ -377,7 +450,7 @@
     def _():
         single(shaped_half, shaped_half, YS).wait_recv()
 
-    transposed(inner_v, shaped_half, is_rx, ip_rx, I_S, I_P)
+    transposed(inner_v, shaped_half, is_rx, ix_rx, ip_rx, I_S)
 
     def dot_copy(slot, d):
         return pltpu.make_async_remote_copy(
@@ -428,13 +501,24 @@
 
     @pl.when(active)
     def _():
-        sent(half1, A1, False)
-        sent(half1, A1S, True)
-        sent(half2, A2, False)
-        sent(half2, A2S, True)
-        sent(own3, A3, False)
-        sent(own3, A3S, True)
-        sent(own3, A3Y, True)
+        def gathered(half, ch):
+            def forwarded(j, to):
+                rc(half.at[column(j)], half.at[p], ch + to, column(j), p, sib).wait_send()
+
+            loop(1, rungs, lambda j: forwarded(j, 0))
+            loop(0, rungs, lambda j: forwarded(j, 1))
+            sent(half, ch + 2)
+
+        gathered(half1, A1)
+        gathered(half2, A2)
+        gathered(own3, A3)
+
+        def over_y(k):
+            @pl.when(jnp.logical_not(over_x(k)))
+            def _():
+                rc(own3.at[k], own3.at[k], A3Y, k, k, sib).wait_send()
+
+        loop(0, pairs, over_y)
         single(normal_half, normal_half, YN).wait_send()
         single(shaped_half, shaped_half, YS).wait_send()
         single(image, image, YI).wait_send()
@@ -450,8 +534,17 @@
     def _():
         single(ytx1, yrx1, Y1).wait_send()
         single(ytx2, yrx2, Y2).wait_send()
-        sent(oth3, A3O, True)
-        sent(ys, NY, True)
+        sent(oth3, A3O)
+
+        def over_x_sent(j):
+            k = column(j)
+
+            @pl.when(lax.rem(k // 2, 2) == 1)
+            def _():
+                rc(oth3.at[k], oth3.at[k], A3OX, k, k, sib).wait_send()
+
+        loop(0, rungs, over_x_sent)
+        sent(ys, NY)
 
 
 def update(image, factors, iterate, residual, direction, next_iterate, next_residual, next_direction):
@@ -485,7 +578,7 @@
             pltpu.VMEM((targets, count), f32), pltpu.VMEM((targets, count), bf16),
             block, block, block, block, block, block,
             half, pltpu.VMEM((pairs, targets, own), f32), half, half,
-            half, half, half, half, half, half, half,
+            half, half, half, half, half, half, half, half, half, half,
             pltpu.VMEM((targets, own), bf16), pltpu.VMEM((targets, own), bf16),
             pltpu.VMEM((max(groups // 2, 1), targets, own) if groups > 2 else (1, 8, 128), f32),
             pltpu.VMEM((n, 8, 128), f32),

time: 110 us -> 115 us (1.045)
  Pallas kernels: 109 us -> 114 us
    pallas_call x1, Pallas kernels: 107 us -> 112 us  [local(): pl.pallas_call(functools.partial(kernel, groups, n, count * groups * n),...]
where the time goes in v4:
time: 115 us
  Pallas kernels  114 us (99%)
    pallas_call x1, Pallas kernels, local(): pl.pallas_call(functools.partial(kernel, groups, n, count * groups * n),...  112 us

profile of v4, /device:TPU:0, one launch (start us, length us, event | category | flops | bytes accessed | tf_op | source)
XLA Modules:
  0.0 115.0 jit_solution(11116185503304680588)
XLA Ops:
  0.6 112.5 %shard_map.94 = (f32[64,512]{1,0:T(8,128)}, f32[64,128]{1,0:T(8,128)}) custom-call(bf16[2048,128]{1,0:T(8,128)(2,1)} %points_hbm.1, bf16[8192,128]{1,0:T(8,128)(2,1)} %centers_hbm.1, bf16[512,8192]{1,0:T(8,128)(2,1)} %inner_hbm.1, bf16[512,8192]{1,0:T(8,128)(2,1)} %outer_hbm.1, f32[64,512]{1,0:T(8,128)} %residual.3, f32[64,512]{1,0:T(8,128)} %direction.3), custom_call_target="tpu_custom_call" | custom-call | flops 8589934592 | bytes 16777216 | tf_op jit(solution)/shard_map/pallas_call | solution.py:568
  113.1 1.9 %shard_map.95 = (f32[64,512]{1,0:T(8,128)}, f32[64,512]{1,0:T(8,128)}, f32[64,512]{1,0:T(8,128)}) custom-call(f32[64,512]{1,0:T(8,128)} %get-tuple-element.5.image, f32[64,128]{1,0:T(8,128)} %get-tuple-element.6.factors, f32[64,512]{1,0:T(8,128)} %iterate.1, f32[64,512]{1,0:T(8,128)} %residual.3, f32[64,512]{1,0:T(8,128)} %direction.3), custom_call_target="tpu_custom_call" | custom-call | tf_op jit(solution)/shard_map/pallas_call | solution.py:596

commit v5 on v2

--- a/solution.py
+++ b/solution.py
@@ -204,6 +204,13 @@
     spread(own3, A3)
     fit[...] = jnp.zeros_like(fit)
 
+    def fit_add(block, b):
+        wide = jnp.concatenate([block.astype(f32), jnp.zeros((128 - targets, own), f32)], axis=0)
+        weights = wide.T.astype(bf16)
+        for i in range(points_hbm.shape[0] // tile):
+            at = slice(i * tile, (i + 1) * tile)
+            fit[at, :] += mm(gram[b, at, :], weights)
+
     def fit_step(s):
         k, k1, k2 = back(s), back(s - 1), back(s - 2)
 
@@ -222,7 +229,7 @@
 
         @pl.when(s < pairs)
         def _():
-            fit[...] += nt(own3[k], gram[2 * k + q])
+            fit_add(own3[k], 2 * k + q)
 
         @pl.when(s >= 2)
         def _():
@@ -230,10 +237,10 @@
             def _():
                 rc(oth3.at[k2], oth3.at[k2], A3O, k2, k2, sib).wait_recv()
 
-            fit[...] += nt(oth3[k2], gram[2 * k2 + 1 - q])
+            fit_add(oth3[k2], 2 * k2 + 1 - q)
 
     loop(0, pairs + 2, fit_step)
-    fit_half[...] = fit[...].astype(bf16)
+    fit_half[...] = fit[...].T[:targets, :].astype(bf16)
 
     def normal_step(s):
         k, k1, k2 = ahead(s), ahead(s - 1 + pairs), ahead(s - 2 + pairs)
@@ -482,7 +489,7 @@
             pltpu.VMEM((count, dims), bf16), pltpu.VMEM(centers.shape, bf16),
             pltpu.VMEM((count, 2 * dims), bf16), pltpu.VMEM((2 * dims, own), bf16),
             half, half, half, half,
-            pltpu.VMEM((targets, count), f32), pltpu.VMEM((targets, count), bf16),
+            pltpu.VMEM((count, 128), f32), pltpu.VMEM((targets, count), bf16),
             block, block, block, block, block, block,
             half, pltpu.VMEM((pairs, targets, own), f32), half, half,
             half, half, half, half, half, half, half,

time: 110 us -> 110 us (level)
  no operation moved by 1% of the time
where the time goes in v5:
time: 110 us
  Pallas kernels  110 us (100%)
    pallas_call x1, Pallas kernels, local(): pl.pallas_call(functools.partial(kernel, groups, n, count * groups * n),...  108 us

profile of v5, /device:TPU:0, one launch (start us, length us, event | category | flops | bytes accessed | tf_op | source)
XLA Modules:
  0.0 110.3 jit_solution(6546621570697128861)
XLA Ops:
  0.6 107.7 %shard_map.94 = (f32[64,512]{1,0:T(8,128)}, f32[64,128]{1,0:T(8,128)}) custom-call(bf16[2048,128]{1,0:T(8,128)(2,1)} %points_hbm.1, bf16[8192,128]{1,0:T(8,128)(2,1)} %centers_hbm.1, bf16[512,8192]{1,0:T(8,128)(2,1)} %inner_hbm.1, bf16[512,8192]{1,0:T(8,128)(2,1)} %outer_hbm.1, f32[64,512]{1,0:T(8,128)} %residual.3, f32[64,512]{1,0:T(8,128)} %direction.3), custom_call_target="tpu_custom_call" | custom-call | flops 8589934592 | bytes 16777216 | tf_op jit(solution)/shard_map/pallas_call | solution.py:482
  108.4 1.9 %shard_map.95 = (f32[64,512]{1,0:T(8,128)}, f32[64,512]{1,0:T(8,128)}, f32[64,512]{1,0:T(8,128)}) custom-call(f32[64,512]{1,0:T(8,128)} %get-tuple-element.5.image, f32[64,128]{1,0:T(8,128)} %get-tuple-element.6.factors, f32[64,512]{1,0:T(8,128)} %iterate.1, f32[64,512]{1,0:T(8,128)} %residual.3, f32[64,512]{1,0:T(8,128)} %direction.3), custom_call_target="tpu_custom_call" | custom-call | tf_op jit(solution)/shard_map/pallas_call | solution.py:510

commit v6 on v2

--- a/solution.py
+++ b/solution.py
@@ -114,7 +114,6 @@
         @pl.when(2 * h + q != g)
         def _():
             pl.semaphore_signal(barrier, inc=1, device_id=(2 * h + q, r), device_id_type=MESH)
-    pl.semaphore_wait(barrier, 2 * n - 1 + groups // 2 - 1)
 
     def spread(half, ch):
         @pl.when(active)
@@ -145,7 +144,6 @@
             at = slice(i * tile, (i + 1) * tile)
             gram[b, at, :] = jnp.exp(mm(points_aug[at, :], centers_aug[...])).astype(bf16)
 
-    spread(half1, A1)
     points_in.wait()
     for i in range(points_hbm.shape[0] // tile):
         at = slice(i * tile, (i + 1) * tile)
@@ -155,6 +153,16 @@
         points_aug[at, dims:] = norm_columns(wide, 0, 3).astype(bf16)
     centers_in.wait()
 
+    unit = n // 16
+    marks = [0, unit, 6 * unit, 8 * unit, 13 * unit, 15 * unit, n]
+
+    def gram_blocks(place):
+        loop(marks[place], marks[place + 1], gram_block)
+
+    gram_blocks(0)
+    pl.semaphore_wait(barrier, 2 * n - 1 + groups // 2 - 1)
+    spread(half1, A1)
+
     acc[...] = jnp.zeros_like(acc)
 
     def inner_step(s):
@@ -162,7 +170,10 @@
         take(half1, A1, s, k)
         slab(inner_hbm, inner_v, 0, k).wait()
         acc[...] += nt(half1[k], inner_v[k])
-        gram_block(s)
+
+        @pl.when(s < marks[2] - marks[1])
+        def _():
+            gram_block(marks[1] + s)
 
     loop(0, pairs, inner_step)
 
@@ -170,6 +181,8 @@
     def _():
         ytx1[...] = acc[...]
         single(ytx1, yrx1, Y1).start()
+
+    gram_blocks(2)
 
     @pl.when(active)
     def _():
@@ -186,7 +199,10 @@
         take(half2, A2, s, k)
         slab(outer_hbm, outer_v, 1, k).wait()
         acc[...] += nt(half2[k], outer_v[k])
-        gram_block(pairs + s)
+
+        @pl.when(s < marks[4] - marks[3])
+        def _():
+            gram_block(marks[3] + s)
 
     loop(0, pairs, outer_step)
 
@@ -194,6 +210,8 @@
     def _():
         ytx2[...] = acc[...]
         single(ytx2, yrx2, Y2).start()
+
+    gram_blocks(4)
 
     @pl.when(active)
     def _():
@@ -202,6 +220,7 @@
         rc(own3.at[p], oth3.at[p], A3Y, p, p, across).start()
 
     spread(own3, A3)
+    gram_blocks(5)
     fit[...] = jnp.zeros_like(fit)
 
     def fit_step(s):

time: 110 us -> 107 us (0.973)
  Pallas kernels: 109 us -> 106 us
    pallas_call x1, Pallas kernels: 107 us -> 104 us  [local(): pl.pallas_call(functools.partial(kernel, groups, n, count * groups * n),...]
where the time goes in v6:
time: 107 us
  Pallas kernels  106 us (99%)
    pallas_call x1, Pallas kernels, local(): pl.pallas_call(functools.partial(kernel, groups, n, count * groups * n),...  104 us

profile of v6, /device:TPU:0, one launch (start us, length us, event | category | flops | bytes accessed | tf_op | source)
XLA Modules:
  0.0 106.5 jit_solution(11714637264156488812)
XLA Ops:
  0.6 103.9 %shard_map.94 = (f32[64,512]{1,0:T(8,128)}, f32[64,128]{1,0:T(8,128)}) custom-call(bf16[2048,128]{1,0:T(8,128)(2,1)} %points_hbm.1, bf16[8192,128]{1,0:T(8,128)(2,1)} %centers_hbm.1, bf16[512,8192]{1,0:T(8,128)(2,1)} %inner_hbm.1, bf16[512,8192]{1,0:T(8,128)(2,1)} %outer_hbm.1, f32[64,512]{1,0:T(8,128)} %residual.3, f32[64,512]{1,0:T(8,128)} %direction.3), custom_call_target="tpu_custom_call" | custom-call | flops 8589934592 | bytes 16777216 | tf_op jit(solution)/shard_map/pallas_call | solution.py:494
  104.6 1.9 %shard_map.95 = (f32[64,512]{1,0:T(8,128)}, f32[64,512]{1,0:T(8,128)}, f32[64,512]{1,0:T(8,128)}) custom-call(f32[64,512]{1,0:T(8,128)} %get-tuple-element.5.image, f32[64,128]{1,0:T(8,128)} %get-tuple-element.6.factors, f32[64,512]{1,0:T(8,128)} %iterate.1, f32[64,512]{1,0:T(8,128)} %residual.3, f32[64,512]{1,0:T(8,128)} %direction.3), custom_call_target="tpu_custom_call" | custom-call | tf_op jit(solution)/shard_map/pallas_call | solution.py:522

commit v7 on v6

--- a/solution.py
+++ b/solution.py
@@ -1,4 +1,5 @@
 import functools
+import math
 
 import jax
 import jax.numpy as jnp
@@ -36,6 +37,16 @@
     held = jnp.where(lane == first + 2, low, held)
     held = jnp.where((lane >= other) & (lane < other + 3), 1.0, held)
     return held
+
+
+def exponential(power):
+    y = jnp.maximum(power * math.log2(math.e), -160.0)
+    coarse = y.astype(bf16)
+    left = (y - coarse.astype(f32)).astype(bf16)
+    scale = jnp.exp2(coarse)
+    ln2 = math.log(2.0)
+    series = left * (left * bf16(0.5 * ln2 * ln2) + bf16(ln2))
+    return scale + scale * series
 
 
 def kernel(
@@ -142,7 +153,7 @@
         centers_aug[dims:, :] = norm_columns(wide, 3, 0).T.astype(bf16)
         for i in range(points_hbm.shape[0] // tile):
             at = slice(i * tile, (i + 1) * tile)
-            gram[b, at, :] = jnp.exp(mm(points_aug[at, :], centers_aug[...])).astype(bf16)
+            gram[b, at, :] = exponential(mm(points_aug[at, :], centers_aug[...]))
 
     points_in.wait()
     for i in range(points_hbm.shape[0] // tile):

time: 107 us -> 111 us (1.037)
  Pallas kernels: 106 us -> 110 us
    pallas_call x1, Pallas kernels: 104 us -> 108 us  [local(): pl.pallas_call(functools.partial(kernel, groups, n, count * groups * n),...]
where the time goes in v7:
time: 111 us
  Pallas kernels  110 us (99%)
    pallas_call x1, Pallas kernels, local(): pl.pallas_call(functools.partial(kernel, groups, n, count * groups * n),...  108 us

profile of v7, /device:TPU:0, one launch (start us, length us, event | category | flops | bytes accessed | tf_op | source)
XLA Modules:
  0.0 110.7 jit_solution(17107416408844877184)
XLA Ops:
  0.6 108.1 %shard_map.94 = (f32[64,512]{1,0:T(8,128)}, f32[64,128]{1,0:T(8,128)}) custom-call(bf16[2048,128]{1,0:T(8,128)(2,1)} %points_hbm.1, bf16[8192,128]{1,0:T(8,128)(2,1)} %centers_hbm.1, bf16[512,8192]{1,0:T(8,128)(2,1)} %inner_hbm.1, bf16[512,8192]{1,0:T(8,128)(2,1)} %outer_hbm.1, f32[64,512]{1,0:T(8,128)} %residual.3, f32[64,512]{1,0:T(8,128)} %direction.3), custom_call_target="tpu_custom_call" | custom-call | flops 8589934592 | bytes 16777216 | tf_op jit(solution)/shard_map/pallas_call | solution.py:505
  108.7 1.9 %shard_map.95 = (f32[64,512]{1,0:T(8,128)}, f32[64,512]{1,0:T(8,128)}, f32[64,512]{1,0:T(8,128)}) custom-call(f32[64,512]{1,0:T(8,128)} %get-tuple-element.5.image, f32[64,128]{1,0:T(8,128)} %get-tuple-element.6.factors, f32[64,512]{1,0:T(8,128)} %iterate.1, f32[64,512]{1,0:T(8,128)} %residual.3, f32[64,512]{1,0:T(8,128)} %direction.3), custom_call_target="tpu_custom_call" | custom-call | tf_op jit(solution)/shard_map/pallas_call | solution.py:533
